TPU v7x, 128 devices: a whole 4x4x4 slice. The times are simulated.
128 devices in a mesh: ctx: 16 (over y, x), head: 8 (over z, core).
Axes of the slice: x: 4, y: 4, z: 4, core: 2. Of those that a mesh axis runs over, the one named last changes fastest.
Arguments:
- input_queries: bfloat16 [16384, 6144], P(('ctx', 'head')), may hold values from -6 to 6
- input_keys: bfloat16 [16384, 1024], P(('ctx', 'head')), may hold values from -6 to 6
- input_values: bfloat16 [16384, 1024], P(('ctx', 'head')), may hold values from -6 to 6
- cotangent: bfloat16 [16384, 6144], P(('ctx', 'head')), may hold values from -6 to 6
- block_list: int32 [32, 8], replicated, may hold values from 0 to 31, as said below
- block_count: int32 [32], replicated, may hold values from 1 to 8, as said below
Outputs:
- attn_out: bfloat16 [16384, 6144], P(('ctx', 'head'))
- grad_query: bfloat16 [16384, 6144], P(('ctx', 'head'))
- key_gradient: bfloat16 [16384, 1024], P(('ctx', 'head'))
- value_gradient: bfloat16 [16384, 1024], P(('ctx', 'head'))
Inputs may be any that keep to these rules, and one draw needn't show every extreme that they name: `block_list`: row b lists entry 0 = b itself, then distinct blocks of other ctx indices up to position block_count[b] - 1, block c belonging to ctx index c // 2; entries from position block_count[b] on repeat b and are unused. The rows of the 2 query blocks of one ctx index together name at most one block of any other ctx index. `block_count`: query block 0 lists 8 blocks.
All inputs are finite; a program needn't handle non-finite values.
Results may differ from a plain program's by a relative error of at most 0.015.
Values may be sent and summed in bfloat16 or wider, within the bound.
A program may use at most 128 MiB of HBM per device.

v0:
```python
import jax
import jax.numpy as jnp
from jax import lax
from jax.sharding import PartitionSpec as P

QUERY_HEADS = 48
KEY_VALUE_HEADS = 8
HEAD_WIDTH = 128
BLOCK_TOKENS = 512


NEG_FILL = -1e30


def shards(input_queries, input_keys, input_values, cotangent, block_list, block_count):
    ctx_rank = lax.axis_index("ctx")
    query_loc, key_loc, value_loc, cot_loc = (
        lax.all_to_all(input_queries, "head", split_axis=1, concat_axis=0, tiled=True),
        lax.all_to_all(input_keys, "head", split_axis=1, concat_axis=0, tiled=True),
        lax.all_to_all(input_values, "head", split_axis=1, concat_axis=0, tiled=True),
        lax.all_to_all(cotangent, "head", split_axis=1, concat_axis=0, tiled=True),
    )
    tok_ctx = query_loc.shape[0]
    own_blocks = tok_ctx // BLOCK_TOKENS
    kv_local = key_loc.shape[1] // HEAD_WIDTH
    group_width = QUERY_HEADS // KEY_VALUE_HEADS
    half_width = kv_local * HEAD_WIDTH
    score_scale = HEAD_WIDTH ** (-0.5)
    own_table = jnp.concatenate([key_loc, value_loc], axis=1).reshape(
        own_blocks, BLOCK_TOKENS, 2 * half_width
    )
    blocked_queries = query_loc.reshape(own_blocks, BLOCK_TOKENS, kv_local, group_width, HEAD_WIDTH)
    cotangent_blocks = cot_loc.reshape(own_blocks, BLOCK_TOKENS, kv_local, group_width, HEAD_WIDTH)
    first_block = ctx_rank * own_blocks
    my_lists = lax.dynamic_slice_in_dim(block_list, first_block, own_blocks, 0)
    my_counts = lax.dynamic_slice_in_dim(block_count, first_block, own_blocks, 0)
    kv_table = lax.all_gather(own_table, "ctx", axis=0, tiled=True)

    def tile_parts(slot_id):
        tile_data = lax.dynamic_index_in_dim(kv_table, slot_id, 0, keepdims=False)
        tile_keys = tile_data[:, :half_width].reshape(BLOCK_TOKENS, kv_local, HEAD_WIDTH)
        tile_values = tile_data[:, half_width:].reshape(BLOCK_TOKENS, kv_local, HEAD_WIDTH)
        return (tile_keys, tile_values)

    def one_block(grad_table, inputs):
        query_b, cot_b, slot_ids, live_count = inputs
        stat_shape = (kv_local, group_width, BLOCK_TOKENS)

        def tile_scores(tile_keys):
            return (
                jnp.einsum("qgjd,kgd->gjqk", query_b, tile_keys, preferred_element_type=jnp.float32)
                * score_scale
            )

        def scan_stats(step_id, running):
            top_score, row_total = running
            tile_keys, tile_values = tile_parts(slot_ids[step_id])
            scores = tile_scores(tile_keys)
            new_top = jnp.maximum(top_score, jnp.max(scores, axis=-1))
            row_total = row_total * jnp.exp(top_score - new_top) + jnp.sum(
                jnp.exp(scores - new_top[..., None]), axis=-1
            )
            return (new_top, row_total)

        start_stats = (
            jnp.full(stat_shape, NEG_FILL, jnp.float32),
            jnp.zeros(stat_shape, jnp.float32),
        )
        top_score, row_total = lax.fori_loop(0, live_count, scan_stats, start_stats)
        log_total = top_score + jnp.log(row_total)

        def add_values(step_id, summed):
            tile_keys, tile_values = tile_parts(slot_ids[step_id])
            weights = jnp.exp(tile_scores(tile_keys) - log_total[..., None]).astype(jnp.bfloat16)
            return summed + jnp.einsum(
                "gjqk,kgd->qgjd", weights, tile_values, preferred_element_type=jnp.float32
            )

        out_shape = (BLOCK_TOKENS, kv_local, group_width, HEAD_WIDTH)
        attended = lax.fori_loop(
            0, live_count, add_values, jnp.zeros(out_shape, jnp.float32)
        ).astype(jnp.bfloat16)
        row_delta = jnp.sum(attended.astype(jnp.float32) * cot_b.astype(jnp.float32), axis=-1)
        row_delta = jnp.transpose(row_delta, (1, 2, 0))

        def add_grads(step_id, carried):
            grad_q, table_acc = carried
            slot_id = slot_ids[step_id]
            tile_keys, tile_values = tile_parts(slot_id)
            weights = jnp.exp(tile_scores(tile_keys) - log_total[..., None])
            weights_b = weights.astype(jnp.bfloat16)
            grad_weights = jnp.einsum(
                "qgjd,kgd->gjqk", cot_b, tile_values, preferred_element_type=jnp.float32
            )
            grad_scores = (weights * (grad_weights - row_delta[..., None])).astype(jnp.bfloat16)
            grad_q = grad_q + jnp.einsum(
                "gjqk,kgd->qgjd", grad_scores, tile_keys, preferred_element_type=jnp.float32
            )
            key_gradient_part = (
                jnp.einsum(
                    "gjqk,qgjd->kgd", grad_scores, query_b, preferred_element_type=jnp.float32
                )
                * score_scale
            )
            value_gradient_part = jnp.einsum(
                "gjqk,qgjd->kgd", weights_b, cot_b, preferred_element_type=jnp.float32
            )
            tile_grads = jnp.concatenate(
                [
                    key_gradient_part.reshape(BLOCK_TOKENS, half_width),
                    value_gradient_part.reshape(BLOCK_TOKENS, half_width),
                ],
                axis=1,
            )
            table_acc = table_acc.at[slot_id].add(tile_grads)
            return (grad_q, table_acc)

        grad_q, grad_table = lax.fori_loop(
            0, live_count, add_grads, (jnp.zeros(out_shape, jnp.float32), grad_table)
        )
        return (grad_table, (attended, (grad_q * score_scale).astype(jnp.bfloat16)))

    start_table = jnp.zeros((kv_table.shape[0], BLOCK_TOKENS, 2 * half_width), jnp.float32)
    grad_table, block_outs = lax.scan(
        one_block, start_table, (blocked_queries, cotangent_blocks, my_lists, my_counts)
    )
    own_grads = lax.psum_scatter(
        grad_table.astype(jnp.bfloat16), "ctx", scatter_dimension=0, tiled=True
    ).astype(jnp.float32)
    grad_key_loc = own_grads[:, :, :half_width].reshape(tok_ctx, half_width).astype(jnp.bfloat16)
    grad_value_loc = own_grads[:, :, half_width:].reshape(tok_ctx, half_width).astype(jnp.bfloat16)
    attn_loc = block_outs[0].reshape(tok_ctx, kv_local * group_width * HEAD_WIDTH)
    grad_query_loc = block_outs[1].reshape(tok_ctx, kv_local * group_width * HEAD_WIDTH)
    attn_out, grad_query, key_gradient, value_gradient = (
        lax.all_to_all(attn_loc, "head", split_axis=0, concat_axis=1, tiled=True),
        lax.all_to_all(grad_query_loc, "head", split_axis=0, concat_axis=1, tiled=True),
        lax.all_to_all(grad_key_loc, "head", split_axis=0, concat_axis=1, tiled=True),
        lax.all_to_all(grad_value_loc, "head", split_axis=0, concat_axis=1, tiled=True),
    )
    return (attn_out, grad_query, key_gradient, value_gradient)


def solution(mesh):
    placed = (
        P(("ctx", "head"), None),
        P(("ctx", "head"), None),
        P(("ctx", "head"), None),
        P(("ctx", "head"), None),
        P(),
        P(),
    )
    return jax.shard_map(
        shards,
        mesh=mesh,
        in_specs=placed,
        out_specs=(
            P(("ctx", "head"), None),
            P(("ctx", "head"), None),
            P(("ctx", "head"), None),
            P(("ctx", "head"), None),
        ),
        check_vma=False,
    )
```

profile of v0, /device:TPU:1, one launch (start us, length us, event | category | flops | bytes accessed | tf_op | source)
XLA Modules:
  0.0 657.1 jit_solution(2847681913517316232)
XLA Ops:
  8.9 6.8 %all-to-all-start.1 = ((bf16[128,8,128]{2,0,1:T(8,128)(2,1)}), bf16[128,8,128]{2,0,1:T(8,128)(2,1)S(1)}, u32[]{:S(2)}, u32[]{:S(2)}) async-start(bf16[128,8,128]{2,0,1:T(8,128)(2,1)} %copy_bitcast_fusion.1), calls=%async_computation.1 | async-start | bytes 524288 | tf_op jit(solution)/shard_map/all_to_all | solution.py:19
  16.7 5.5 all-to-all-done.1
  22.2 9.9 %all_to_all.134 = bf16[128,8,128]{2,0,1:T(8,128)(2,1)S(1)} all-to-all(bf16[128,8,128]{2,0,1:T(8,128)(2,1)S(1)} %copy_bitcast_fusion), channel_id=1, replica_groups=mesh['ctx'=16,'head'=8] {'head'}, dimensions={1} | all-to-all | bytes 524288 | tf_op jit(solution)/shard_map/all_to_all | solution.py:20
  34.6 4.7 all-to-all-start
  40.9 19.1 %all-to-all-done = bf16[128,8,768]{0,2,1:T(8,128)(2,1)S(1)} async-done(((bf16[128,8,768]{0,2,1:T(8,128)(2,1)}), bf16[128,8,768]{0,2,1:T(8,128)(2,1)S(1)}, u32[]{:S(2)}, u32[]{:S(2)}) %all-to-all-start) | async-done | bytes 1572896 | tf_op jit(solution)/shard_map/all_to_all | solution.py:18
  60.0 4.4 all-to-all-start.3
  66.7 2.7 reshape.175
  70.9 14.2 %all-to-all-done.3 = bf16[128,8,768]{0,2,1:T(8,128)(2,1)S(1)} async-done(((bf16[128,8,768]{0,2,1:T(8,128)(2,1)}), bf16[128,8,768]{0,2,1:T(8,128)(2,1)S(1)}, u32[]{:S(2)}, u32[]{:S(2)}) %all-to-all-start.3) | async-done | bytes 1572896 | tf_op jit(solution)/shard_map/all_to_all | solution.py:21
  88.2 15.5 %all-gather.2.cloned.1.call-done = bf16[32,512,256]{2,1,0:T(8,128)(2,1)} async-done(((bf16[2,512,256]{2,1,0:T(8,128)(2,1)}), bf16[32,512,256]{2,1,0:T(8,128)(2,1)}) %all-gather.2.cloned.1.call-update) | async-done | bytes 8388624 | tf_op jit(solution)/shard_map/all_gather | solution.py:37
  103.6 7.9 %broadcast_in_dim.15 = f32[32,512,256]{1,2,0:T(8,128)} broadcast(f32[]{:T(128)} %constant.96.clone.1), dimensions={} | broadcast | bytes 16777220 | tf_op jit(solution)/shard_map/broadcast_in_dim | solution.py:123
  111.5 241.7 %while.52 = (s32[]{:T(128)}, f32[32,512,256]{1,2,0:T(8,128)}, bf16[2,512,1,6,128]{1,4,3,2,0:T(8,128)(2,1)}, bf16[2,512,1,6,128]{1,4,3,2,0:T(8,128)(2,1)}, s32[2]...) while((s32[]{:T(128)}, f32[32,512,256]{1,2,0:T(8,128)}, ...), condition=%wide.region_11.12_spmd, body=%wide.region_0.11_spmd.sunk | while | flops 3250788352 | bytes 77101416 | solution.py:124
  113.8 48.5 %while.53 = (s32[]{:T(128)}, f32[1,6,512]{2,1,0:T(8,128)S(1)}, f32[1,6,512]{2,1,0:T(8,128)S(1)}, s32[]{:T(128)}, s32[8]{0:T(128)S(1)}, /*index=5*/bf16[32,512,25...) while((s32[]{:T(128)}, f32[1,6,512]{2,1,0:T(8,128)S(1)}, ...), condition=%wide.region_4.4_spmd, body=%wide.region_1.3_spmd.sunk | while | flops 410523648 | bytes 14184649 | solution.py:69
  162.4 46.3 %while.54 = (s32[]{:T(128)}, f32[512,1,6,128]{0,3,2,1:T(8,128)S(1)}, s32[]{:T(128)}, s32[8]{0:T(128)S(1)}, bf16[32,512,256]{2,1,0:T(8,128)(2,1)}, /*index=5*/bf1...) while((s32[]{:T(128)}, ...), condition=%wide.region_6.6_spmd, body=%wide.region_5.5_spmd.sunk | while | flops 810418176 | bytes 4731081 | solution.py:80
  210.9 105.3 %while.55 = (s32[]{:T(128)}, f32[512,1,6,128]{0,3,2,1:T(8,128)S(1)}, f32[32,512,256]{1,2,0:T(8,128)}, s32[]{:T(128)}, s32[8]{0:T(128)S(1)}, /*index=5*/bf16[32,5...) while((s32[]{:T(128)}, ...), condition=%wide.region_10.10_spmd, body=%wide.region_8.9_spmd.sunk | while | flops 2026700800 | bytes 37664004 | solution.py:118
  234.5 2.6 fusion.80
  260.7 2.6 fusion.80
  300.0 2.6 fusion.80
  316.2 2.9 fusion.65
  321.3 6.6 %while.53 = (s32[]{:T(128)}, f32[1,6,512]{2,1,0:T(8,128)S(1)}, f32[1,6,512]{2,1,0:T(8,128)S(1)}, s32[]{:T(128)}, s32[8]{0:T(128)S(1)}, /*index=5*/bf16[32,512,25...) while((s32[]{:T(128)}, f32[1,6,512]{2,1,0:T(8,128)S(1)}, ...), condition=%wide.region_4.4_spmd, body=%wide.region_1.3_spmd.sunk | while | flops 410523648 | bytes 14184649 | solution.py:69
  328.1 6.3 while.54
  336.7 13.7 %while.55 = (s32[]{:T(128)}, f32[512,1,6,128]{0,3,2,1:T(8,128)S(1)}, f32[32,512,256]{1,2,0:T(8,128)}, s32[]{:T(128)}, s32[8]{0:T(128)S(1)}, /*index=5*/bf16[32,5...) while((s32[]{:T(128)}, ...), condition=%wide.region_10.10_spmd, body=%wide.region_8.9_spmd.sunk | while | flops 2026700800 | bytes 37664004 | solution.py:118
  350.4 2.9 fusion.65
  353.2 13.8 %copy.94 = bf16[32,512,256]{2,1,0:T(8,128)(2,1)} copy(f32[32,512,256]{1,2,0:T(8,128)} %get-tuple-element.854) | data formatting | bytes 25165824 | tf_op jit(solution)/shard_map/while | solution.py:124
  372.8 5.1 all-to-all-start.5
  377.9 3.0 copy.90
  383.2 2.8 copy.91
  385.9 12.7 %all-to-all-done.5 = bf16[8,128,768]{1,2,0:T(8,128)(2,1)S(1)} async-done(((bf16[8,128,768]{1,2,0:T(8,128)(2,1)}), bf16[8,128,768]{1,2,0:T(8,128)(2,1)S(1)}, u32[]{:S(2)}, u32[]{:S(2)}) %all-to-all-start.5) | async-done | bytes 1572896 | tf_op jit(solution)/shard_map/all_to_all | solution.py:136
  398.6 5.0 all-to-all-start.4
  403.7 220.3 %reduce-scatter.2.cloned.1.call-done = bf16[2,512,256]{2,1,0:T(8,128)(2,1)} async-done(((bf16[32,512,256]{2,1,0:T(8,128)(2,1)}), bf16[2,512,256]{2,1,0:T(8,128)(2,1)}) %reduce-scatter.2.cloned.1.call-update) | async-done | bytes 524304 | tf_op jit(solution)/shard_map/reduce_scatter | solution.py:127
  625.7 12.6 %all_to_all.135 = bf16[8,128,128]{2,1,0:T(8,128)(2,1)S(1)} all-to-all(bf16[8,128,128]{2,1,0:T(8,128)(2,1)S(1)} %bitcast.301), channel_id=1, replica_groups=mesh['ctx'=16,'head'=8] {'head'}, dimensions={0} | all-to-all | bytes 524288 | tf_op jit(solution)/shard_map/all_to_all | solution.py:137
  638.3 4.4 all-to-all-start.7
  644.2 2.6 copy.97
  (239 shorter events, 187.2 us)
Async XLA Ops:
  7.2 1.0 copy-start
  7.2 25.8 %copy-start.3 = (bf16[128,6144]{1,0:T(8,128)(2,1)S(1)}, bf16[128,6144]{1,0:T(8,128)(2,1)}, u32[]{:S(2)}) copy-start(bf16[128,6144]{1,0:T(8,128)(2,1)} %param.16) | copy-start | bytes 4718596
  8.9 13.3 %all-to-all-start.1 = ((bf16[128,8,128]{2,0,1:T(8,128)(2,1)}), bf16[128,8,128]{2,0,1:T(8,128)(2,1)S(1)}, u32[]{:S(2)}, u32[]{:S(2)}) async-start(bf16[128,8,128]{2,0,1:T(8,128)(2,1)} %copy_bitcast_fusion.1), calls=%async_computation.1 | async-start | bytes 524288 | tf_op jit(solution)/shard_map/all_to_all | solution.py:19
  15.7 88.0 %all-gather.2.cloned.1.call-start = ((), (), s32[]{:S(2)}) async-start(), calls=%async_computation.9 | async-start | bytes 8912896 | tf_op jit(solution)/shard_map/all_gather | solution.py:37
  34.6 4.7 copy-start.4
  34.6 25.4 %all-to-all-start = ((bf16[128,8,768]{0,2,1:T(8,128)(2,1)}), bf16[128,8,768]{0,2,1:T(8,128)(2,1)S(1)}, u32[]{:S(2)}, u32[]{:S(2)}) async-start(bf16[128,8,768]{0,2,1:T(8,128)(2,1)} %bitcast.50), calls=%async_computation | async-start | bytes 3145728 | tf_op jit(solution)/shard_map/all_to_all | solution.py:18
  39.2 25.1 %copy-start.8 = (s32[32]{0:T(128)S(1)}, s32[32]{0:T(128)}, u32[]{:S(2)}) copy-start(s32[32]{0:T(128)} %param.21) | copy-start | bytes 388
  39.2 25.2 %copy-start.7 = (s32[32,8]{0,1:T(8,128)S(1)}, s32[32,8]{0,1:T(8,128)}, u32[]{:S(2)}) copy-start(s32[32,8]{0,1:T(8,128)} %param.20) | copy-start | bytes 3076
  60.0 25.1 %all-to-all-start.3 = ((bf16[128,8,768]{0,2,1:T(8,128)(2,1)}), bf16[128,8,768]{0,2,1:T(8,128)(2,1)S(1)}, u32[]{:S(2)}, u32[]{:S(2)}) async-start(bf16[128,8,768]{0,2,1:T(8,128)(2,1)} %bitcast.56), calls=%async_computation.3 | async-start | bytes 3145728 | tf_op jit(solution)/shard_map/all_to_all | solution.py:21
  64.3 559.6 %reduce-scatter.2.cloned.1.call-start = ((), (), s32[]{:S(2)}) async-start(), calls=%async_computation.10 | async-start | bytes 8912896 | tf_op jit(solution)/shard_map/reduce_scatter | solution.py:127
  88.2 23.4 %copy-start.6 = (s32[3]{0:T(128)S(1)}, s32[3]{0:T(128)}, u32[]{:S(2)}) copy-start(s32[3]{0:T(128)} %constant.87.clone.3) | copy-start | bytes 40
  208.8 2.0 copy-start.2
  334.5 2.0 copy-start.2
  367.1 1.4 copy-start.5
  372.8 25.8 %all-to-all-start.5 = ((bf16[8,128,768]{1,2,0:T(8,128)(2,1)}), bf16[8,128,768]{1,2,0:T(8,128)(2,1)S(1)}, u32[]{:S(2)}, u32[]{:S(2)}) async-start(bf16[8,128,768]{1,2,0:T(8,128)(2,1)} %copy.93), calls=%async_computation.5 | async-start | bytes 3145728 | tf_op jit(solution)/shard_map/all_to_all | solution.py:136
  398.6 227.1 %all-to-all-start.4 = ((bf16[8,128,768]{1,2,0:T(8,128)(2,1)}), bf16[8,128,768]{1,2,0:T(8,128)(2,1)}, u32[]{:S(2)}, u32[]{:S(2)}) async-start(bf16[8,128,768]{1,2,0:T(8,128)(2,1)} %copy.91), calls=%async_computation.4 | async-start | bytes 3145728 | tf_op jit(solution)/shard_map/all_to_all | solution.py:135
  638.3 10.9 %all-to-all-start.7 = ((bf16[8,128,128]{2,1,0:T(8,128)(2,1)}), bf16[8,128,128]{2,1,0:T(8,128)(2,1)S(1)}, u32[]{:S(2)}, u32[]{:S(2)}) async-start(bf16[8,128,128]{2,1,0:T(8,128)(2,1)} %bitcast.65), calls=%async_computation.8 | async-start | bytes 524288 | tf_op jit(solution)/shard_map/all_to_all | solution.py:138
  642.6 7.6 %copy-start.1 = (bf16[128,1024]{1,0:T(8,128)(2,1)S(1)}, bf16[128,1024]{1,0:T(8,128)(2,1)}, u32[]{:S(2)}) copy-start(bf16[128,1024]{1,0:T(8,128)(2,1)} %param.17) | copy-start | bytes 786436
Sparse Core Ops, SparseCore 0:
  33.1 70.4 all-gather.1
  367.2 256.6 reduce-scatter.1
where the time goes:
time: 649 us; the launch traced here: 657 us
  waiting for transfers between devices  289 us (45%)
  local copies, waits for them, and re-layouts  106 us (16%)
  matrix products  75.9 us (12%)
  loops' own time  69.5 us (11%)
  other arithmetic  49.8 us (8%)
  starting transfers between devices  30.3 us (5%)
  blocking collectives  22.5 us (3%)
  between operations  14.1 us (2%)
    reduce_scatter x1, waiting for transfers between devices, shards(): lax.psum_scatter(grad_table.astype(jnp.bfloat16), 'ctx', scatter_dimensio...  220 us
    squeeze x27, local copies, waits for them, and re-layouts, tile_parts(): tile_data = lax.dynamic_index_in_dim(kv_table, slot_id, 0, keepdims=False)  26.2 us
    another operation x2, loops' own time, one_block(): lax.fori_loop(0, live_count, add_grads, (jnp.zeros(out_shape, jnp.float32...  24.5 us
    scatter-add x9, other arithmetic, add_grads(): table_acc = table_acc.at[slot_id].add(tile_grads)  23.1 us
    another operation x2, loops' own time, one_block(): top_score, row_total = lax.fori_loop(0, live_count, scan_stats, start_stats)  22.5 us
    another operation x2, loops' own time, one_block(): lax.fori_loop(0, live_count, add_values, jnp.zeros(out_shape, jnp.float32))  22.3 us
    while x5, local copies, waits for them, and re-layouts, shards(): lax.scan(one_block, start_table, (blocked_queries, cotangent_blocks, my_l...  21.4 us
    all_to_all x1, waiting for transfers between devices, shards(): lax.all_to_all(input_queries, 'head', split_axis=1, concat_axis=0, tiled=...  19.1 us
  transfers between devices with their start and end apart: 8, of which 7 were waited for; matrix products, arithmetic and copies ran while one was open for 5% of the time, Pallas kernels for 0%

commit v1 on v0

v1 whole, which is shorter than its diff:
```python
import jax
import jax.numpy as jnp
import numpy as np
from jax import lax
from jax.experimental import pallas as pl
from jax.experimental.pallas import tpu as pltpu
from jax.sharding import PartitionSpec as P

HEAD_WIDTH=128; BLOCK_TOKENS=512; GROUP=6
SCALE=HEAD_WIDTH**-0.5
LOG2E=1.4426950408889634
NT=(((1,),(1,)),((),()))
T=BLOCK_TOKENS; D=HEAD_WIDTH

def attn_kernel(meta, q_ref, cot_ref, kv_hbm, out_ref, dq_ref, send_ref, own_ref,
                kv, pst, mst, acc, run, dqa, sems):
    f32=jnp.float32; bf=jnp.bfloat16
    def fetch(n):
        return pltpu.make_async_copy(kv_hbm.at[meta[n]], kv.at[n], sems.at[n])
    for n in range(16):
        @pl.when(n % 8 < meta[48 + n//8])
        def _(): fetch(n).start()
    for b in range(2):
        rows=slice(b*T,(b+1)*T)
        cnt=meta[48+b]
        acc[...]=jnp.zeros_like(acc)
        run[0]=jnp.full((8,T),-1e30,f32)
        run[1]=jnp.zeros((8,T),f32)
        def fwd(i, _):
            fetch(b*8+i).wait()
            k=kv[b*8+i,:,:D]; vt=kv[b*8+i,:,D:].T
            for j in range(GROUP):
                qj=q_ref[rows,j*D:(j+1)*D]
                s=lax.dot_general(k,qj,NT,preferred_element_type=f32)
                mx=jnp.max(s,axis=0,keepdims=True)*(SCALE*LOG2E)
                p=jnp.exp2(s*(SCALE*LOG2E)-mx)
                li=jnp.sum(p,axis=0,keepdims=True)
                pb=p.astype(bf)
                pst[i,:,j*T:(j+1)*T]=pb
                ot=jnp.dot(vt,pb,preferred_element_type=f32)
                mo=run[0,j:j+1]; mn=jnp.maximum(mo,mx)
                al=jnp.exp2(mo-mn); be=jnp.exp2(mx-mn)
                mst[i,j:j+1]=mx
                run[0,j:j+1]=mn
                run[1,j:j+1]=run[1,j:j+1]*al+li*be
                acc[j]=acc[j]*al+ot*be
            return 0
        lax.fori_loop(0,cnt,fwd,0)
        for j in range(GROUP):
            o=(acc[j]/run[1,j:j+1]).astype(bf)
            out_ref[rows,j*D:(j+1)*D]=o.T
            ct=cot_ref[rows,j*D:(j+1)*D].T
            run[2,j:j+1]=jnp.sum(o.astype(f32)*ct.astype(f32),axis=0,keepdims=True)
        dqa[...]=jnp.zeros_like(dqa)
        def bwd(i,_):
            k=kv[b*8+i,:,:D]; v=kv[b*8+i,:,D:]; kt=k.T
            dk=jnp.zeros((T,D),f32); dv=jnp.zeros((T,D),f32)
            for j in range(GROUP):
                qj=q_ref[rows,j*D:(j+1)*D]; cj=cot_ref[rows,j*D:(j+1)*D]
                dp=lax.dot_general(v,cj,NT,preferred_element_type=f32)
                r=jnp.exp2(mst[i,j:j+1]-run[0,j:j+1])/run[1,j:j+1]
                pn=pst[i,:,j*T:(j+1)*T].astype(f32)*r
                ds=(pn*(dp-run[2,j:j+1])).astype(bf)
                dqa[j]+=jnp.dot(kt,ds,preferred_element_type=f32)
                dk+=jnp.dot(ds,qj,preferred_element_type=f32)
                dv+=jnp.dot(pn.astype(bf),cj,preferred_element_type=f32)
            dk=dk*SCALE
            d=meta[32+b*8+i]; sh=meta[16+b*8+i]
            @pl.when(i==0)
            def _():
                own_ref[b,:,:D]=dk; own_ref[b,:,D:]=dv
            @pl.when(jnp.logical_and(i>0, sh==0))
            def _():
                send_ref[d,:,:D]=dk.astype(bf); send_ref[d,:,D:]=dv.astype(bf)
            @pl.when(jnp.logical_and(i>0, sh!=0))
            def _():
                send_ref[d,:,:D]=(send_ref[d,:,:D].astype(f32)+dk).astype(bf)
                send_ref[d,:,D:]=(send_ref[d,:,D:].astype(f32)+dv).astype(bf)
            return 0
        lax.fori_loop(0,cnt,bwd,0)
        for j in range(GROUP):
            dq_ref[rows,j*D:(j+1)*D]=(dqa[j]*SCALE).astype(bf).T

def attn(meta,q,cot,kvt):
    f32=jnp.float32; bf=jnp.bfloat16
    V=pl.BlockSpec(memory_space=pltpu.VMEM)
    return pl.pallas_call(attn_kernel,
        out_shape=(jax.ShapeDtypeStruct((2*T,GROUP*D),bf),)*2+(jax.ShapeDtypeStruct((16,T,2*D),bf),jax.ShapeDtypeStruct((2,T,2*D),f32)),
        in_specs=[pl.BlockSpec(memory_space=pltpu.SMEM),V,V,pl.BlockSpec(memory_space=pl.ANY)],
        out_specs=(V,)*4,
        scratch_shapes=[pltpu.VMEM((16,T,2*D),bf),pltpu.VMEM((8,T,GROUP*T),bf),pltpu.VMEM((8,8,T),f32),
            pltpu.VMEM((GROUP,D,T),f32),pltpu.VMEM((3,8,T),f32),pltpu.VMEM((GROUP,D,T),f32),pltpu.SemaphoreType.DMA((16,))],
        compiler_params=pltpu.CompilerParams(vmem_limit_bytes=62*1024*1024),
        )(meta,q,cot,kvt)


def plan(block_list, ctx):
    rows = lax.dynamic_slice_in_dim(block_list, 2 * ctx, 2, 0)
    owner = rows // 2
    shared = jnp.any(owner[1][:, None] == owner[0][None, :], axis=1).astype(jnp.int32)
    return rows, owner, shared


def heads_in(x):
    width = x.shape[1] // 8
    x = jnp.transpose(x.reshape(x.shape[0], 8, width), (1, 0, 2))
    return lax.all_to_all(x, "head", split_axis=0, concat_axis=0, tiled=True).reshape(-1, width)


def heads_out(x):
    width = x.shape[1]
    x = lax.all_to_all(x.reshape(8, -1, width), "head", split_axis=0, concat_axis=0, tiled=True)
    return jnp.transpose(x, (1, 0, 2)).reshape(-1, 8 * width)


def shards(input_queries, input_keys, input_values, cotangent, block_list, block_count):
    ctx = lax.axis_index("ctx")
    keys, values = heads_in(input_keys), heads_in(input_values)
    own_table = jnp.concatenate([keys, values], axis=1).reshape(2, T, 2 * D)
    table = lax.all_gather(own_table, "ctx", axis=0, tiled=True)
    queries, cot = heads_in(input_queries), heads_in(cotangent)
    rows, owner, shared = plan(block_list, ctx)
    counts = lax.dynamic_slice_in_dim(block_count, 2 * ctx, 2, 0)
    meta = jnp.concatenate(
        [rows.reshape(16), jnp.zeros(8, jnp.int32), shared, owner.reshape(16), counts, jnp.zeros(14, jnp.int32)]
    )
    out, dq, send, own = attn(meta, queries, cot, table)
    got = lax.all_to_all(send, "ctx", split_axis=0, concat_axis=0, tiled=True)
    mine = 2 * ctx + jnp.arange(2)
    named = jnp.any(block_list.reshape(16, 16)[:, :, None] == mine[None, None, :], axis=1)
    named = jnp.logical_and(named, (jnp.arange(16) != ctx)[:, None])
    parts = jnp.where(named[:, :, None, None], got[:, None], jnp.zeros((), jnp.bfloat16))
    grads = (own + jnp.sum(parts.astype(jnp.float32), axis=0)).astype(jnp.bfloat16).reshape(2 * T, 2 * D)
    return heads_out(out), heads_out(dq), heads_out(grads[:, :D]), heads_out(grads[:, D:])


def solution(mesh):
    spec = P(("ctx", "head"), None)
    return jax.shard_map(
        shards,
        mesh=mesh,
        in_specs=(spec,) * 4 + (P(), P()),
        out_specs=(spec,) * 4,
        check_vma=False,
    )
```

time: 649 us -> 378 us (0.58); the launches traced: 657 us -> 377 us
  waiting for transfers between devices: 289 us -> 139 us
  local copies, waits for them, and re-layouts: 106 us -> 14.6 us
  matrix products: 75.9 us -> 0 us
  Pallas kernels: 0 us -> 74.8 us
  loops' own time: 69.5 us -> 0 us
  starting transfers between devices: 30.3 us -> 83.1 us
  other arithmetic: 49.8 us -> 5.8 us
  blocking collectives: 22.5 us -> 45.6 us
    reduce_scatter x1 -> x0, waiting for transfers between devices: 220 us -> none  [shards(): lax.psum_scatter(grad_table.astype(jnp.bfloat16), 'ctx', scatter_dimensio...]
    dot_general x63 -> x0, matrix products: 75.9 us -> none  [the longest x18 17.6 us: tile_scores(): jnp.einsum('qgjd,kgd->gjqk', query_b, tile_keys, preferred_element_type=j...]
    pallas_call x0 -> x1, Pallas kernels: none -> 74.8 us  [attn(): pl.pallas_call(attn_kernel, out_shape=(jax.ShapeDtypeStruct((2 * T, GROUP...]
    another operation x7 -> x0, loops' own time: 69.5 us -> none  [the longest x2 24.5 us: one_block(): lax.fori_loop(0, live_count, add_grads, (jnp.zeros(out_shape, jnp.float32...]
    all_to_all x6, waiting for transfers between devices: 52.8 us -> 122 us  [the longest x1 60.9 us: shards(): got = lax.all_to_all(send, 'ctx', split_axis=0, concat_axis=0, tiled=True)]
    all_to_all x6, starting transfers between devices: 30.3 us -> 83.1 us  [the longest x1 55.7 us: shards(): got = lax.all_to_all(send, 'ctx', split_axis=0, concat_axis=0, tiled=True)]
    squeeze x31 -> x0, local copies, waits for them, and re-layouts: 28.6 us -> none  [the longest x27 26.2 us: tile_parts(): tile_data = lax.dynamic_index_in_dim(kv_table, slot_id, 0, keepdims=False)]
    scatter-add x9 -> x0, other arithmetic: 23.1 us -> none  [add_grads(): table_acc = table_acc.at[slot_id].add(tile_grads)]
  transfers between devices with their start and end apart: 8 -> 7, of which waited for: 7 -> 7; matrix products, arithmetic and copies ran while one was open for 5% -> 4% of each run, Pallas kernels for 0% -> 0%
where the time goes in v1:
time: 378 us; the launch traced here: 377 us
  waiting for transfers between devices  139 us (37%)
  starting transfers between devices  83.1 us (22%)
  Pallas kernels  74.8 us (20%)
  blocking collectives  45.6 us (12%)
  local copies, waits for them, and re-layouts  14.6 us (4%)
  between operations  14.1 us (4%)
  other arithmetic  5.8 us (2%)
    pallas_call x1, Pallas kernels, attn(): pl.pallas_call(attn_kernel, out_shape=(jax.ShapeDtypeStruct((2 * T, GROUP...  74.8 us
    all_to_all x1, waiting for transfers between devices, shards(): got = lax.all_to_all(send, 'ctx', split_axis=0, concat_axis=0, tiled=True)  60.9 us
    all_to_all x1, starting transfers between devices, shards(): got = lax.all_to_all(send, 'ctx', split_axis=0, concat_axis=0, tiled=True)  55.7 us
    all_to_all x3, waiting for transfers between devices, heads_in(): lax.all_to_all(x, 'head', split_axis=0, concat_axis=0, tiled=True)  44.4 us
    all_to_all x2, blocking collectives, heads_out(): lax.all_to_all(x.reshape(8, -1, width), 'head', split_axis=0, concat_axis...  35.6 us
    all_gather x1, waiting for transfers between devices, shards(): table = lax.all_gather(own_table, 'ctx', axis=0, tiled=True)  17 us
    all_to_all x2, waiting for transfers between devices, heads_out(): lax.all_to_all(x.reshape(8, -1, width), 'head', split_axis=0, concat_axis...  17 us
    all_to_all x3, starting transfers between devices, heads_in(): lax.all_to_all(x, 'head', split_axis=0, concat_axis=0, tiled=True)  16.6 us
  transfers between devices with their start and end apart: 7, of which 7 were waited for; matrix products, arithmetic and copies ran while one was open for 4% of the time, Pallas kernels for 0%

profile of v1, /device:TPU:1, one launch (start us, length us, event | category | flops | bytes accessed | tf_op | source)
XLA Modules:
  0.0 377.2 jit_solution(17552334281691323743)
XLA Ops:
  7.2 0.9 copy-done
  8.1 0.8 bitcast_bitcast_fusion.3
  8.9 6.9 %all-to-all-start.2 = ((bf16[8,128,128]{2,1,0:T(8,128)(2,1)}), bf16[8,128,128]{2,1,0:T(8,128)(2,1)S(1)}, u32[]{:S(2)}, u32[]{:S(2)}) async-start(bf16[8,128,128]{2,1,0:T(8,128)(2,1)} %bitcast_bitcast_fusion.3), calls=%async_computation.2 | async-start | bytes 524288 | tf_op jit(solution)/shard_map/all_to_all | solution.py:107
  15.8 1.0 bitcast_bitcast_fusion.2
  16.8 5.5 %all-to-all-done.2 = bf16[8,128,128]{2,1,0:T(8,128)(2,1)S(1)} async-done(((bf16[8,128,128]{2,1,0:T(8,128)(2,1)}), bf16[8,128,128]{2,1,0:T(8,128)(2,1)S(1)}, u32[]{:S(2)}, u32[]{:S(2)}) %all-to-all-start.2) | async-done | bytes 262176 | tf_op jit(solution)/shard_map/all_to_all | solution.py:107
  22.3 9.9 %all_to_all.45 = bf16[8,128,128]{2,1,0:T(8,128)(2,1)S(1)} all-to-all(bf16[8,128,128]{2,1,0:T(8,128)(2,1)S(1)} %bitcast_bitcast_fusion.2), channel_id=1, replica_groups=mesh['ctx'=16,'head'=8] {'head'}, dimensions={0} | all-to-all | bytes 524288 | tf_op jit(solution)/shard_map/all_to_all | solution.py:107
  32.3 0.9 pad_maximum_fusion
  33.2 1.2 copy.78
  34.4 4.7 %all-to-all-start = ((bf16[8,128,768]{2,1,0:T(8,128)(2,1)}), bf16[8,128,768]{2,1,0:T(8,128)(2,1)S(1)}, u32[]{:S(2)}, u32[]{:S(2)}) async-start(bf16[8,128,768]{2,1,0:T(8,128)(2,1)} %bitcast.48), calls=%async_computation | async-start | bytes 3145728 | tf_op jit(solution)/shard_map/all_to_all | solution.py:107
  39.1 1.2 copy.77
  40.3 19.5 %all-to-all-done = bf16[8,128,768]{2,1,0:T(8,128)(2,1)S(1)} async-done(((bf16[8,128,768]{2,1,0:T(8,128)(2,1)}), bf16[8,128,768]{2,1,0:T(8,128)(2,1)S(1)}, u32[]{:S(2)}, u32[]{:S(2)}) %all-to-all-start) | async-done | bytes 1572896 | tf_op jit(solution)/shard_map/all_to_all | solution.py:107
  59.8 1.1 copy-done.1
  61.0 5.0 %all-to-all-start.1 = ((bf16[8,128,768]{2,1,0:T(8,128)(2,1)}), bf16[8,128,768]{2,1,0:T(8,128)(2,1)}, u32[]{:S(2)}, u32[]{:S(2)}) async-start(bf16[8,128,768]{2,1,0:T(8,128)(2,1)} %bitcast.46), calls=%async_computation.1 | async-start | bytes 3145728 | tf_op jit(solution)/shard_map/all_to_all | solution.py:107
  66.9 0.6 concatenate.11.meta
  67.5 19.4 %all-to-all-done.1 = bf16[8,128,768]{2,1,0:T(8,128)(2,1)} async-done(((bf16[8,128,768]{2,1,0:T(8,128)(2,1)}), bf16[8,128,768]{2,1,0:T(8,128)(2,1)}, u32[]{:S(2)}, u32[]{:S(2)}) %all-to-all-start.1) | async-done | bytes 1572896 | tf_op jit(solution)/shard_map/all_to_all | solution.py:107
  86.8 17.0 %all-gather.2.cloned.1.call-done.kv_hbm = bf16[32,512,256]{2,1,0:T(8,128)(2,1)} async-done(((bf16[2,512,256]{2,1,0:T(8,128)(2,1)}), bf16[32,512,256]{2,1,0:T(8,128)(2,1)}) %all-gather.2.cloned.1.call-update) | async-done | bytes 8388624 | tf_op jit(solution)/shard_map/all_gather | solution.py:120
  103.8 74.8 %shard_map.93 = (bf16[1024,768]{1,0:T(8,128)(2,1)}, bf16[1024,768]{1,0:T(8,128)(2,1)}, bf16[16,512,256]{2,1,0:T(8,128)(2,1)}, f32[2,512,256]{2,1,0:T(8,128)}) custom-call(s32[64]{0:T(128)} %concatenate.11.meta, bf16[1024,768]{1,0:T(8,128)(2,1)} %bitcast.50, bf16[1024,768]{1,0:T(8,128)(2,1)} %bitcast.3.cot_ref, ...), custom_call_target="tpu_custom_call" | custom-call | tf_op jit(solution)/shard_map/pallas_call | solution.py:87
  178.6 25.9 %all_to_all.46 = bf16[8,128,768]{2,1,0:T(8,128)(2,1)S(1)} all-to-all(bf16[8,128,768]{2,1,0:T(8,128)(2,1)} %bitcast.56), channel_id=1, replica_groups=mesh['ctx'=16,'head'=8] {'head'}, dimensions={0} | all-to-all | bytes 3145728 | tf_op jit(solution)/shard_map/all_to_all | solution.py:112
  204.5 55.7 %all-to-all-start.6 = ((bf16[16,512,256]{2,1,0:T(8,128)(2,1)}), bf16[16,512,256]{2,1,0:T(8,128)(2,1)}, u32[]{:S(2)}, u32[]{:S(2)}) async-start(bf16[16,512,256]{2,1,0:T(8,128)(2,1)} %get-tuple-element.11), calls=%async_computation.6 | async-start | bytes 8388608 | tf_op jit(solution)/shard_map/all_to_all | solution.py:128
  260.4 0.2 compare_reduce_fusion
  260.6 60.9 %all-to-all-done.6 = bf16[16,512,256]{2,1,0:T(8,128)(2,1)} async-done(((bf16[16,512,256]{2,1,0:T(8,128)(2,1)}), bf16[16,512,256]{2,1,0:T(8,128)(2,1)}, u32[]{:S(2)}, u32[]{:S(2)}) %all-to-all-start.6) | async-done | bytes 4194336 | tf_op jit(solution)/shard_map/all_to_all | solution.py:128
  321.4 6.4 %all-to-all-start.5 = ((bf16[8,128,768]{2,1,0:T(8,128)(2,1)}), bf16[8,128,768]{2,1,0:T(8,128)(2,1)}, u32[]{:S(2)}, u32[]{:S(2)}) async-start(bf16[8,128,768]{2,1,0:T(8,128)(2,1)} %bitcast.10), calls=%async_computation.5 | async-start | bytes 3145728 | tf_op jit(solution)/shard_map/all_to_all | solution.py:112
  327.9 4.3 %convert_reduce_fusion = f32[2,512,256]{2,1,0:T(8,128)S(1)} fusion(pred[16,2]{1,0:T(8,128)(4,1)S(1)} %copy.62, bf16[16,512,256]{2,1,0:T(8,128)(2,1)} %all-to-all-done.6), kind=kLoop, calls=%fused_computation | loop fusion | flops 12320768 | bytes 5242912 | tf_op jit(solution)/shard_map/reduce_sum | solution.py:133
  332.4 0.7 fusion.2
  333.1 15.5 %all-to-all-done.5 = bf16[8,128,768]{2,1,0:T(8,128)(2,1)} async-done(((bf16[8,128,768]{2,1,0:T(8,128)(2,1)}), bf16[8,128,768]{2,1,0:T(8,128)(2,1)}, u32[]{:S(2)}, u32[]{:S(2)}) %all-to-all-start.5) | async-done | bytes 1572896 | tf_op jit(solution)/shard_map/all_to_all | solution.py:112
  348.7 9.8 %all_to_all.47 = bf16[8,128,128]{2,1,0:T(8,128)(2,1)S(1)} all-to-all(bf16[8,128,128]{2,1,0:T(8,128)(2,1)S(1)} %bitcast.60), channel_id=1, replica_groups=mesh['ctx'=16,'head'=8] {'head'}, dimensions={0} | all-to-all | bytes 524288 | tf_op jit(solution)/shard_map/all_to_all | solution.py:112
  358.4 4.4 %all-to-all-start.8 = ((bf16[8,128,128]{2,1,0:T(8,128)(2,1)}), bf16[8,128,128]{2,1,0:T(8,128)(2,1)S(1)}, u32[]{:S(2)}, u32[]{:S(2)}) async-start(bf16[8,128,128]{2,1,0:T(8,128)(2,1)} %bitcast.16), calls=%async_computation.8 | async-start | bytes 524288 | tf_op jit(solution)/shard_map/all_to_all | solution.py:112
  362.8 1.3 copy.71
  364.1 2.7 copy.72
  367.0 0.9 copy.65
  367.8 1.5 all-to-all-done.8
  369.5 0.9 copy.66
  (34 shorter events, 1.7 us)
Async XLA Ops:
  7.2 1.0 copy-start
  8.9 24.3 %copy-start.2 = (bf16[128,6144]{1,0:T(8,128)(2,1)S(1)}, bf16[128,6144]{1,0:T(8,128)(2,1)}, u32[]{:S(2)}) copy-start(bf16[128,6144]{1,0:T(8,128)(2,1)} %param.6) | copy-start | bytes 4718596
  8.9 13.4 %all-to-all-start.2 = ((bf16[8,128,128]{2,1,0:T(8,128)(2,1)}), bf16[8,128,128]{2,1,0:T(8,128)(2,1)S(1)}, u32[]{:S(2)}, u32[]{:S(2)}) async-start(bf16[8,128,128]{2,1,0:T(8,128)(2,1)} %bitcast_bitcast_fusion.3), calls=%async_computation.2 | async-start | bytes 524288 | tf_op jit(solution)/shard_map/all_to_all | solution.py:107
  15.8 88.0 %all-gather.2.cloned.1.call-start = ((), (), s32[]{:S(2)}) async-start(), calls=%async_computation.9 | async-start | bytes 8912896 | tf_op jit(solution)/shard_map/all_gather | solution.py:120
  34.4 4.7 %copy-start.3 = (bf16[128,6144]{1,0:T(8,128)(2,1)S(1)}, bf16[128,6144]{1,0:T(8,128)(2,1)}, u32[]{:S(2)}) copy-start(bf16[128,6144]{1,0:T(8,128)(2,1)} %param.9) | copy-start | bytes 4718596
  34.4 25.4 %all-to-all-start = ((bf16[8,128,768]{2,1,0:T(8,128)(2,1)}), bf16[8,128,768]{2,1,0:T(8,128)(2,1)S(1)}, u32[]{:S(2)}, u32[]{:S(2)}) async-start(bf16[8,128,768]{2,1,0:T(8,128)(2,1)} %bitcast.48), calls=%async_computation | async-start | bytes 3145728 | tf_op jit(solution)/shard_map/all_to_all | solution.py:107
  59.8 1.1 copy-start.1
  59.8 6.2 %copy-start.5 = (s32[32,8]{0,1:T(8,128)S(1)}, s32[32,8]{0,1:T(8,128)}, u32[]{:S(2)}) copy-start(s32[32,8]{0,1:T(8,128)} %param.10) | copy-start | bytes 3076
  59.8 7.0 %copy-start.6 = (s32[32]{0:T(128)S(1)}, s32[32]{0:T(128)}, u32[]{:S(2)}) copy-start(s32[32]{0:T(128)} %param.11) | copy-start | bytes 388
  61.0 25.9 %all-to-all-start.1 = ((bf16[8,128,768]{2,1,0:T(8,128)(2,1)}), bf16[8,128,768]{2,1,0:T(8,128)(2,1)}, u32[]{:S(2)}, u32[]{:S(2)}) async-start(bf16[8,128,768]{2,1,0:T(8,128)(2,1)} %bitcast.46), calls=%async_computation.1 | async-start | bytes 3145728 | tf_op jit(solution)/shard_map/all_to_all | solution.py:107
  204.5 116.9 %all-to-all-start.6 = ((bf16[16,512,256]{2,1,0:T(8,128)(2,1)}), bf16[16,512,256]{2,1,0:T(8,128)(2,1)}, u32[]{:S(2)}, u32[]{:S(2)}) async-start(bf16[16,512,256]{2,1,0:T(8,128)(2,1)} %get-tuple-element.11), calls=%async_computation.6 | async-start | bytes 8388608 | tf_op jit(solution)/shard_map/all_to_all | solution.py:128
  321.4 27.2 %all-to-all-start.5 = ((bf16[8,128,768]{2,1,0:T(8,128)(2,1)}), bf16[8,128,768]{2,1,0:T(8,128)(2,1)}, u32[]{:S(2)}, u32[]{:S(2)}) async-start(bf16[8,128,768]{2,1,0:T(8,128)(2,1)} %bitcast.10), calls=%async_computation.5 | async-start | bytes 3145728 | tf_op jit(solution)/shard_map/all_to_all | solution.py:112
  327.9 4.3 %copy-start.4 = (f32[2,512,256]{2,1,0:T(8,128)S(1)}, f32[2,512,256]{2,1,0:T(8,128)}, u32[]{:S(2)}) copy-start(f32[2,512,256]{2,1,0:T(8,128)} %get-tuple-element.10) | copy-start | bytes 3145732
  358.4 10.9 %all-to-all-start.8 = ((bf16[8,128,128]{2,1,0:T(8,128)(2,1)}), bf16[8,128,128]{2,1,0:T(8,128)(2,1)S(1)}, u32[]{:S(2)}, u32[]{:S(2)}) async-start(bf16[8,128,128]{2,1,0:T(8,128)(2,1)} %bitcast.16), calls=%async_computation.8 | async-start | bytes 524288 | tf_op jit(solution)/shard_map/all_to_all | solution.py:112
Sparse Core Ops, SparseCore 0:
  33.3 70.5 all-gather.1

commit v2 on v1

--- a/solution.py
+++ b/solution.py
@@ -1,6 +1,5 @@
 import jax
 import jax.numpy as jnp
-import numpy as np
 from jax import lax
 from jax.experimental import pallas as pl
 from jax.experimental.pallas import tpu as pltpu
@@ -94,44 +93,271 @@
         )(meta,q,cot,kvt)
 
 
-def plan(block_list, ctx):
+CTX = 16
+HEADS = 8
+MESH = pl.DeviceIdType.MESH
+QW = GROUP * D
+
+
+def greet(ctx, head):
+    barrier = pltpu.get_barrier_semaphore()
+
+    def ctx_peer(n, _):
+        pl.semaphore_signal(barrier, inc=1, device_id=(lax.rem(ctx + n, CTX), head), device_id_type=MESH)
+        return 0
+
+    def head_peer(n, _):
+        pl.semaphore_signal(barrier, inc=1, device_id=(ctx, lax.rem(head + n, HEADS)), device_id_type=MESH)
+        return 0
+
+    lax.fori_loop(1, CTX, ctx_peer, 0)
+    lax.fori_loop(1, HEADS, head_peer, 0)
+    pl.semaphore_wait(barrier, CTX + HEADS - 2)
+
+
+def cols(index, width):
+    return pl.ds(pl.multiple_of(index * width, width), width)
+
+
+def spread_kernel(pick, q_ref, k_ref, v_ref, c_ref, qh_ref, ch_ref, table_ref,
+                  kv_own, stage, head_send, head_recv, ctx_send, ctx_recv, local_sem):
+    ctx, head = lax.axis_index("ctx"), lax.axis_index("head")
+    greet(ctx, head)
+    tokens = k_ref.shape[0]
+    arrays = (
+        (k_ref, lambda s: kv_own.at[cols(s, tokens), :D], D),
+        (v_ref, lambda s: kv_own.at[cols(s, tokens), D:], D),
+        (q_ref, lambda s: qh_ref.at[cols(s, tokens)], QW),
+        (c_ref, lambda s: ch_ref.at[cols(s, tokens)], QW),
+    )
+
+    def send(a, to, frm):
+        ref, place, width = arrays[a]
+        return pltpu.make_async_remote_copy(
+            ref.at[:, cols(to, width)], place(frm), head_send.at[a, to], head_recv.at[a, frm],
+            device_id=(ctx, to), device_id_type=MESH)
+
+    def keep(a):
+        ref, place, width = arrays[a]
+        return pltpu.make_async_copy(ref.at[:, cols(head, width)], place(head), local_sem.at[a])
+
+    def start_kv(n, _):
+        to = lax.rem(head + n, HEADS)
+        send(0, to, head).start()
+        send(1, to, head).start()
+        return 0
+
+    def start_q(n, _):
+        to = lax.rem(head + n, HEADS)
+        send(2, to, head).start()
+        send(3, to, head).start()
+        return 0
+
+    for a in range(4):
+        keep(a).start()
+    lax.fori_loop(1, HEADS, start_kv, 0)
+    lax.fori_loop(1, HEADS, start_q, 0)
+
+    def take_kv(n, _):
+        frm = lax.rem(head + n, HEADS)
+        send(0, frm, frm).wait_recv()
+        send(1, frm, frm).wait_recv()
+        return 0
+
+    keep(0).wait()
+    keep(1).wait()
+    lax.fori_loop(1, HEADS, take_kv, 0)
+
+    own = [pltpu.make_async_copy(kv_own.at[b * T:(b + 1) * T], table_ref.at[CTX + b], local_sem.at[4 + b])
+           for b in range(2)]
+    for copy in own:
+        copy.start()
+
+    def push(to, frm):
+        return pltpu.make_async_remote_copy(
+            stage.at[to], table_ref.at[frm], ctx_send.at[to], ctx_recv.at[frm],
+            device_id=(to, head), device_id_type=MESH)
+
+    def start_push(n, _):
+        to = lax.rem(ctx + n, CTX)
+        stage[to] = jnp.where(pick[to] == 1, kv_own[T:], kv_own[:T])
+        push(to, ctx).start()
+        return 0
+
+    lax.fori_loop(1, CTX, start_push, 0)
+
+    def end_push(n, _):
+        peer = lax.rem(ctx + n, CTX)
+        push(peer, ctx).wait_send()
+        push(peer, peer).wait_recv()
+        return 0
+
+    def end_head(n, _):
+        peer = lax.rem(head + n, HEADS)
+        for a in range(4):
+            send(a, peer, head).wait_send()
+        for a in (2, 3):
+            send(a, peer, peer).wait_recv()
+        return 0
+
+    lax.fori_loop(1, HEADS, end_head, 0)
+    keep(2).wait()
+    keep(3).wait()
+    for copy in own:
+        copy.wait()
+    lax.fori_loop(1, CTX, end_push, 0)
+
+
+def spread(pick, q, k, v, cot):
+    bf = jnp.bfloat16
+    any_spec = pl.BlockSpec(memory_space=pl.ANY)
+    return pl.pallas_call(
+        spread_kernel,
+        out_shape=(jax.ShapeDtypeStruct((2 * T, QW), bf), jax.ShapeDtypeStruct((2 * T, QW), bf),
+                   jax.ShapeDtypeStruct((CTX + 2, T, 2 * D), bf)),
+        in_specs=[pl.BlockSpec(memory_space=pltpu.SMEM)] + [any_spec] * 4,
+        out_specs=(any_spec,) * 3,
+        scratch_shapes=[
+            pltpu.VMEM((2 * T, 2 * D), bf),
+            pltpu.VMEM((CTX, T, 2 * D), bf),
+            pltpu.SemaphoreType.DMA((4, HEADS)),
+            pltpu.SemaphoreType.DMA((4, HEADS)),
+            pltpu.SemaphoreType.DMA((CTX,)),
+            pltpu.SemaphoreType.DMA((CTX,)),
+            pltpu.SemaphoreType.DMA((6,)),
+        ],
+        compiler_params=pltpu.CompilerParams(collective_id=0, has_side_effects=True, vmem_limit_bytes=60 * 2**20),
+    )(pick, q, k, v, cot)
+
+
+def collect_kernel(code, out_ref, dq_ref, send_ref, own_ref, o_res, dq_res, dk_res, dv_res,
+                   got, total, grads, ctx_send, ctx_recv, head_send, head_recv, local_sem):
+    f32, bf = jnp.float32, jnp.bfloat16
+    ctx, head = lax.axis_index("ctx"), lax.axis_index("head")
+    greet(ctx, head)
+    tokens = o_res.shape[0]
+    arrays = (
+        (lambda to: out_ref.at[cols(to, tokens)], lambda s: o_res.at[:, cols(s, QW)]),
+        (lambda to: dq_ref.at[cols(to, tokens)], lambda s: dq_res.at[:, cols(s, QW)]),
+        (lambda to: grads.at[cols(to, tokens), :D], lambda s: dk_res.at[:, cols(s, D)]),
+        (lambda to: grads.at[cols(to, tokens), D:], lambda s: dv_res.at[:, cols(s, D)]),
+    )
+
+    def push(to, frm):
+        return pltpu.make_async_remote_copy(
+            send_ref.at[to], got.at[frm], ctx_send.at[to], ctx_recv.at[frm],
+            device_id=(to, head), device_id_type=MESH)
+
+    def send(a, to, frm):
+        source, place = arrays[a]
+        return pltpu.make_async_remote_copy(
+            source(to), place(frm), head_send.at[a, to], head_recv.at[a, frm],
+            device_id=(ctx, to), device_id_type=MESH)
+
+    def keep(a):
+        source, place = arrays[a]
+        return pltpu.make_async_copy(source(head), place(head), local_sem.at[a])
+
+    def start_push(n, _):
+        push(lax.rem(ctx + n, CTX), ctx).start()
+        return 0
+
+    def start_out(n, _):
+        to = lax.rem(head + n, HEADS)
+        send(0, to, head).start()
+        send(1, to, head).start()
+        return 0
+
+    first = pltpu.make_async_copy(own_ref, total, local_sem.at[4])
+    first.start()
+    lax.fori_loop(1, CTX, start_push, 0)
+    lax.fori_loop(1, HEADS, start_out, 0)
+    keep(0).start()
+    keep(1).start()
+    first.wait()
+
+    def add(n, _):
+        frm = lax.rem(ctx + n, CTX)
+        push(frm, frm).wait_recv()
+        mark = code[frm]
+        part = got[frm].astype(f32)
+        total[0] += jnp.where(mark == 1, part, 0.0)
+        total[1] += jnp.where(mark == 2, part, 0.0)
+        return 0
+
+    lax.fori_loop(1, CTX, add, 0)
+    for b in range(2):
+        grads[b * T:(b + 1) * T] = total[b].astype(bf)
+
+    def start_grads(n, _):
+        to = lax.rem(head + n, HEADS)
+        send(2, to, head).start()
+        send(3, to, head).start()
+        return 0
+
+    lax.fori_loop(1, HEADS, start_grads, 0)
+    keep(2).start()
+    keep(3).start()
+
+    def end_push(n, _):
+        push(lax.rem(ctx + n, CTX), ctx).wait_send()
+        return 0
+
+    def end_head(n, _):
+        peer = lax.rem(head + n, HEADS)
+        for a in range(4):
+            send(a, peer, head).wait_send()
+            send(a, peer, peer).wait_recv()
+        return 0
+
+    lax.fori_loop(1, CTX, end_push, 0)
+    lax.fori_loop(1, HEADS, end_head, 0)
+    for a in range(4):
+        keep(a).wait()
+
+
+def collect(code, out, dq, send, own):
+    f32, bf = jnp.float32, jnp.bfloat16
+    any_spec = pl.BlockSpec(memory_space=pl.ANY)
+    tokens = 2 * T // HEADS
+    wide = jax.ShapeDtypeStruct((tokens, HEADS * QW), bf)
+    thin = jax.ShapeDtypeStruct((tokens, HEADS * D), bf)
+    return pl.pallas_call(
+        collect_kernel,
+        out_shape=(wide, wide, thin, thin),
+        in_specs=[pl.BlockSpec(memory_space=pltpu.SMEM)] + [any_spec] * 4,
+        out_specs=(any_spec,) * 4,
+        scratch_shapes=[
+            pltpu.VMEM((CTX, T, 2 * D), bf),
+            pltpu.VMEM((2, T, 2 * D), f32),
+            pltpu.VMEM((2 * T, 2 * D), bf),
+            pltpu.SemaphoreType.DMA((CTX,)),
+            pltpu.SemaphoreType.DMA((CTX,)),
+            pltpu.SemaphoreType.DMA((4, HEADS)),
+            pltpu.SemaphoreType.DMA((4, HEADS)),
+            pltpu.SemaphoreType.DMA((5,)),
+        ],
+        compiler_params=pltpu.CompilerParams(collective_id=1, has_side_effects=True, vmem_limit_bytes=60 * 2**20),
+    )(code, out, dq, send, own)
+
+
+def shards(input_queries, input_keys, input_values, cotangent, block_list, block_count):
+    ctx = lax.axis_index("ctx")
     rows = lax.dynamic_slice_in_dim(block_list, 2 * ctx, 2, 0)
     owner = rows // 2
+    slots = jnp.where(jnp.arange(8)[None, :] == 0, CTX + jnp.arange(2)[:, None], owner)
     shared = jnp.any(owner[1][:, None] == owner[0][None, :], axis=1).astype(jnp.int32)
-    return rows, owner, shared
-
-
-def heads_in(x):
-    width = x.shape[1] // 8
-    x = jnp.transpose(x.reshape(x.shape[0], 8, width), (1, 0, 2))
-    return lax.all_to_all(x, "head", split_axis=0, concat_axis=0, tiled=True).reshape(-1, width)
-
-
-def heads_out(x):
-    width = x.shape[1]
-    x = lax.all_to_all(x.reshape(8, -1, width), "head", split_axis=0, concat_axis=0, tiled=True)
-    return jnp.transpose(x, (1, 0, 2)).reshape(-1, 8 * width)
-
-
-def shards(input_queries, input_keys, input_values, cotangent, block_list, block_count):
-    ctx = lax.axis_index("ctx")
-    keys, values = heads_in(input_keys), heads_in(input_values)
-    own_table = jnp.concatenate([keys, values], axis=1).reshape(2, T, 2 * D)
-    table = lax.all_gather(own_table, "ctx", axis=0, tiled=True)
-    queries, cot = heads_in(input_queries), heads_in(cotangent)
-    rows, owner, shared = plan(block_list, ctx)
     counts = lax.dynamic_slice_in_dim(block_count, 2 * ctx, 2, 0)
     meta = jnp.concatenate(
-        [rows.reshape(16), jnp.zeros(8, jnp.int32), shared, owner.reshape(16), counts, jnp.zeros(14, jnp.int32)]
-    )
+        [slots.reshape(16), jnp.zeros(8, jnp.int32), shared, owner.reshape(16), counts, jnp.zeros(14, jnp.int32)]
+    ).astype(jnp.int32)
+    lists = block_list.reshape(CTX, 16)
+    named = [jnp.any(lists == 2 * ctx + b, axis=1) for b in range(2)]
+    pick = named[1].astype(jnp.int32)
+    code = named[0].astype(jnp.int32) + 2 * pick
+    queries, cot, table = spread(pick, input_queries, input_keys, input_values, cotangent)
     out, dq, send, own = attn(meta, queries, cot, table)
-    got = lax.all_to_all(send, "ctx", split_axis=0, concat_axis=0, tiled=True)
-    mine = 2 * ctx + jnp.arange(2)
-    named = jnp.any(block_list.reshape(16, 16)[:, :, None] == mine[None, None, :], axis=1)
-    named = jnp.logical_and(named, (jnp.arange(16) != ctx)[:, None])
-    parts = jnp.where(named[:, :, None, None], got[:, None], jnp.zeros((), jnp.bfloat16))
-    grads = (own + jnp.sum(parts.astype(jnp.float32), axis=0)).astype(jnp.bfloat16).reshape(2 * T, 2 * D)
-    return heads_out(out), heads_out(dq), heads_out(grads[:, :D]), heads_out(grads[:, D:])
+    return collect(code, out, dq, send, own)
 
 
 def solution(mesh):

time: 378 us -> 305 us (0.81)
  Pallas kernels: 74.8 us -> 294 us
  waiting for transfers between devices: 139 us -> 0 us
  starting transfers between devices: 83.1 us -> 0 us
  blocking collectives: 45.6 us -> 0 us
  between operations: 14.1 us -> 0.71 us
  local copies, waits for them, and re-layouts: 14.6 us -> 7.39 us
    pallas_call x0 -> x2, Pallas kernels: none -> 219 us  [the longest x1 135 us: collect(): pl.pallas_call(collect_kernel, out_shape=(wide, wide, thin, thin), in_spe...]
    all_to_all x6 -> x0, waiting for transfers between devices: 122 us -> none  [the longest x1 60.9 us: shards(): got = lax.all_to_all(send, 'ctx', split_axis=0, concat_axis=0, tiled=True)]
    all_to_all x6 -> x0, starting transfers between devices: 83.1 us -> none  [the longest x1 55.7 us: shards(): got = lax.all_to_all(send, 'ctx', split_axis=0, concat_axis=0, tiled=True)]
    all_to_all x3 -> x0, blocking collectives: 45.6 us -> none  [the longest x2 35.6 us: heads_out(): lax.all_to_all(x.reshape(8, -1, width), 'head', split_axis=0, concat_axis...]
    all_gather x1 -> x0, waiting for transfers between devices: 17 us -> none  [shards(): table = lax.all_gather(own_table, 'ctx', axis=0, tiled=True)]
    reshape x5 -> x1, local copies, waits for them, and re-layouts: 6.6 us -> 0.08 us  [shards(): slots.reshape(16)]
    reduce_sum x1 -> x0, other arithmetic: 4.25 us -> none  [shards(): jnp.sum(parts.astype(jnp.float32), axis=0)]
  transfers between devices with their start and end apart: 7 -> 0, of which waited for: 7 -> 0; matrix products, arithmetic and copies ran while one was open for 4% -> 0% of each run, Pallas kernels for 0% -> 0%
where the time goes in v2:
time: 305 us
  Pallas kernels  294 us (96%)
  local copies, waits for them, and re-layouts  7.39 us (2%)
    pallas_call x1, Pallas kernels, collect(): pl.pallas_call(collect_kernel, out_shape=(wide, wide, thin, thin), in_spe...  135 us
    pallas_call x1, Pallas kernels, spread(): pl.pallas_call(spread_kernel, out_shape=(jax.ShapeDtypeStruct((2 * T, QW)...  84.1 us
    pallas_call x1, Pallas kernels, attn(): pl.pallas_call(attn_kernel, out_shape=(jax.ShapeDtypeStruct((2 * T, GROUP...  74.9 us

profile of v2, /device:TPU:1, one launch (start us, length us, event | category | flops | bytes accessed | tf_op | source)
XLA Modules:
  0.0 304.8 jit_solution(17250170615933420230)
XLA Ops:
  0.6 0.7 compare_reduce_fusion.2
  1.3 0.7 dynamic_slice.7
  2.1 0.1 reduce_or.32
  2.2 0.1 reduce_or.36
  2.3 0.1 reduce_or.45
  2.4 0.1 reduce_or.46
  2.5 0.5 select_add_fusion.code
  3.1 0.5 convert_element_type.11.pick
  3.6 0.8 broadcast_select_fusion
  4.3 0.1 copy.14
  4.4 0.1 reshape.28
  4.5 0.1 copy.15
  4.6 0.2 slice_reduce_fusion.1
  4.8 0.1 reshape.29
  4.8 0.2 compare_reduce_fusion
  5.1 0.6 concatenate.3.meta
  5.7 84.1 %shard_map.93 = (bf16[1024,768]{1,0:T(8,128)(2,1)}, bf16[1024,768]{1,0:T(8,128)(2,1)}, bf16[18,512,256]{2,1,0:T(8,128)(2,1)}) custom-call(s32[16]{0:T(128)} %convert_element_type.11.pick, bf16[128,6144]{1,0:T(8,128)(2,1)} %q_ref.1, bf16[128,1024]{1,0:T(8,128)(2,1)} %k_ref.1, bf16[128,1024]{1,0:T(8,128)(2,1)} %v_ref.1, bf16[128,6144]{1,0:T(8,128)(2,1)} %c_ref.1), custom_call_target="tpu_custom_call" | custom-call | tf_op jit(solution)/shard_map/pallas_call | solution.py:214
  89.7 74.9 %shard_map.94 = (bf16[1024,768]{1,0:T(8,128)(2,1)}, bf16[1024,768]{1,0:T(8,128)(2,1)}, bf16[16,512,256]{2,1,0:T(8,128)(2,1)}, f32[2,512,256]{2,1,0:T(8,128)}) custom-call(s32[64]{0:T(128)} %concatenate.3.meta, bf16[1024,768]{1,0:T(8,128)(2,1)} %get-tuple-element.11.q_ref, bf16[1024,768]{1,0:T(8,128)(2,1)} %get-tuple-element.12.cot_ref, ...), custom_call_target="tpu_custom_call" | custom-call | tf_op jit(solution)/shard_map/pallas_call | solution.py:86
  164.6 134.8 %shard_map.95 = (bf16[128,6144]{1,0:T(8,128)(2,1)}, bf16[128,6144]{1,0:T(8,128)(2,1)}, bf16[128,1024]{1,0:T(8,128)(2,1)}, bf16[128,1024]{1,0:T(8,128)(2,1)}) custom-call(s32[16]{0:T(128)} %select_add_fusion.code, bf16[1024,768]{1,0:T(8,128)(2,1)} %get-tuple-element.14.out_ref, bf16[1024,768]{1,0:T(8,128)(2,1)} %get-tuple-element.15.dq_ref, ...), custom_call_target="tpu_custom_call" | custom-call | tf_op jit(solution)/shard_map/pallas_call | solution.py:325
  299.5 0.0 copy-start
  299.5 2.8 copy.20
  302.3 0.0 copy-done
  302.3 0.0 copy-start.2
  302.3 0.0 copy-start.1
  302.3 1.1 copy.21
  303.4 0.0 copy-done.2
  303.4 0.7 copy.22
  304.1 0.0 copy-done.1
  304.1 0.7 copy.23
  (5 shorter events, 0.0 us)
Async XLA Ops:
  299.5 2.8 copy-start
  302.3 1.1 copy-start.2
  302.3 1.9 copy-start.1

commit v3 on v1

v3 whole, which is shorter than its diff:
```python
import jax
import jax.numpy as jnp
from jax import lax
from jax.experimental import pallas as pl
from jax.experimental.pallas import tpu as pltpu
from jax.sharding import PartitionSpec as P

D = 128
T = 512
GROUP = 6
QW = GROUP * D
SIDE = 4
CTX = SIDE * SIDE
HEADS = 8
MOST = 8
SCALE = D**-0.5
LOG2E = 1.4426950408889634
NT = (((1,), (1,)), ((), ()))
MESH = pl.DeviceIdType.MESH


def attn_kernel(lists, counts, q_ref, cot_ref, kv_hbm, out_ref, dq_ref, send_ref, own_ref,
                kv, pst, mst, acc, run, dqa, sems):
    ctx = lax.axis_index("ctx")

    def owner(b, i):
        return lists[2 * ctx + b, i] // 2

    f32=jnp.float32; bf=jnp.bfloat16
    def fetch(b, i):
        slot = jnp.where(i == 0, CTX + b, owner(b, i))
        return pltpu.make_async_copy(kv_hbm.at[slot], kv.at[b * MOST + i], sems.at[b * MOST + i])

    def prefetch(b):
        def one(i, _):
            fetch(b, i).start()
            return 0
        lax.fori_loop(0, counts[2 * ctx + b], one, 0)

    prefetch(0)
    prefetch(1)
    for b in range(2):
        rows=slice(b*T,(b+1)*T)
        cnt=counts[2*ctx+b]
        acc[...]=jnp.zeros_like(acc)
        run[0]=jnp.full((8,T),-1e30,f32)
        run[1]=jnp.zeros((8,T),f32)
        def fwd(i, _):
            fetch(b, i).wait()
            k=kv[b*8+i,:,:D]; vt=kv[b*8+i,:,D:].T
            for j in range(GROUP):
                qj=q_ref[rows,j*D:(j+1)*D]
                s=lax.dot_general(k,qj,NT,preferred_element_type=f32)
                mx=jnp.max(s,axis=0,keepdims=True)*(SCALE*LOG2E)
                p=jnp.exp2(s*(SCALE*LOG2E)-mx)
                li=jnp.sum(p,axis=0,keepdims=True)
                pb=p.astype(bf)
                pst[i,:,j*T:(j+1)*T]=pb
                ot=jnp.dot(vt,pb,preferred_element_type=f32)
                mo=run[0,j:j+1]; mn=jnp.maximum(mo,mx)
                al=jnp.exp2(mo-mn); be=jnp.exp2(mx-mn)
                mst[i,j:j+1]=mx
                run[0,j:j+1]=mn
                run[1,j:j+1]=run[1,j:j+1]*al+li*be
                acc[j]=acc[j]*al+ot*be
            return 0
        lax.fori_loop(0,cnt,fwd,0)
        for j in range(GROUP):
            o=(acc[j]/run[1,j:j+1]).astype(bf)
            out_ref[rows,j*D:(j+1)*D]=o.T
            ct=cot_ref[rows,j*D:(j+1)*D].T
            run[2,j:j+1]=jnp.sum(o.astype(f32)*ct.astype(f32),axis=0,keepdims=True)
        dqa[...]=jnp.zeros_like(dqa)
        def bwd(i,_):
            k=kv[b*8+i,:,:D]; v=kv[b*8+i,:,D:]; kt=k.T
            dk=jnp.zeros((T,D),f32); dv=jnp.zeros((T,D),f32)
            for j in range(GROUP):
                qj=q_ref[rows,j*D:(j+1)*D]; cj=cot_ref[rows,j*D:(j+1)*D]
                dp=lax.dot_general(v,cj,NT,preferred_element_type=f32)
                r=jnp.exp2(mst[i,j:j+1]-run[0,j:j+1])/run[1,j:j+1]
                pn=pst[i,:,j*T:(j+1)*T].astype(f32)*r
                ds=(pn*(dp-run[2,j:j+1])).astype(bf)
                dqa[j]+=jnp.dot(kt,ds,preferred_element_type=f32)
                dk+=jnp.dot(ds,qj,preferred_element_type=f32)
                dv+=jnp.dot(pn.astype(bf),cj,preferred_element_type=f32)
            dk=dk*SCALE
            d=owner(b, i)
            sh=jnp.int32(0)
            if b == 1:
                for n in range(1, MOST):
                    sh += (owner(0, n) == d).astype(jnp.int32)
            @pl.when(i==0)
            def _():
                own_ref[0,b]=dk; own_ref[1,b]=dv
            @pl.when(jnp.logical_and(i>0, sh==0))
            def _():
                send_ref[d,:,:D]=dk.astype(bf); send_ref[d,:,D:]=dv.astype(bf)
            @pl.when(jnp.logical_and(i>0, sh!=0))
            def _():
                send_ref[d,:,:D]=(send_ref[d,:,:D].astype(f32)+dk).astype(bf)
                send_ref[d,:,D:]=(send_ref[d,:,D:].astype(f32)+dv).astype(bf)
            return 0
        lax.fori_loop(0,cnt,bwd,0)
        for j in range(GROUP):
            dq_ref[rows,j*D:(j+1)*D]=(dqa[j]*SCALE).astype(bf).T

def attn(lists,counts,q,cot,kvt):
    f32=jnp.float32; bf=jnp.bfloat16
    V=pl.BlockSpec(memory_space=pltpu.VMEM)
    return pl.pallas_call(attn_kernel,
        out_shape=(jax.ShapeDtypeStruct((2*T,GROUP*D),bf),)*2+(jax.ShapeDtypeStruct((16,T,2*D),bf),jax.ShapeDtypeStruct((2,2,T,D),f32)),
        in_specs=[pl.BlockSpec(memory_space=pltpu.SMEM)]*2+[V,V,pl.BlockSpec(memory_space=pl.ANY)],
        out_specs=(V,)*4,
        scratch_shapes=[pltpu.VMEM((16,T,2*D),bf),pltpu.VMEM((8,T,GROUP*T),bf),pltpu.VMEM((8,8,T),f32),
            pltpu.VMEM((GROUP,D,T),f32),pltpu.VMEM((3,8,T),f32),pltpu.VMEM((GROUP,D,T),f32),pltpu.SemaphoreType.DMA((16,))],
        compiler_params=pltpu.CompilerParams(vmem_limit_bytes=62*1024*1024),
        )(lists,counts,q,cot,kvt)


def greet(ctx, head):
    barrier = pltpu.get_barrier_semaphore()
    y, x = ctx // SIDE, lax.rem(ctx, SIDE)

    def line(n, _):
        pl.semaphore_signal(barrier, inc=1, device_id=(y * SIDE + lax.rem(x + n, SIDE), head), device_id_type=MESH)
        pl.semaphore_signal(barrier, inc=1, device_id=(lax.rem(y + n, SIDE) * SIDE + x, head), device_id_type=MESH)
        return 0

    def head_peer(n, _):
        pl.semaphore_signal(barrier, inc=1, device_id=(ctx, lax.rem(head + n, HEADS)), device_id_type=MESH)
        return 0

    lax.fori_loop(1, SIDE, line, 0)
    lax.fori_loop(1, HEADS, head_peer, 0)
    pl.semaphore_wait(barrier, 2 * (SIDE - 1) + HEADS - 1)


def cols(index, width):
    return pl.ds(pl.multiple_of(index * width, width), width)


def lists_block(lists, ctx, block):
    hits = jnp.int32(0)
    for b in range(2):
        for i in range(1, MOST):
            hits += (lists[2 * ctx + b, i] == block).astype(jnp.int32)
    return hits > 0


def spread_kernel(lists, q_ref, k_ref, v_ref, c_ref, qh_ref, ch_ref, table_ref,
                  lines, stage, head_send, head_recv, line_send, line_recv, push_send, push_recv, local_sem, fill_sem):
    ctx, head = lax.axis_index("ctx"), lax.axis_index("head")
    y, x = ctx // SIDE, lax.rem(ctx, SIDE)
    here = (x, y)
    greet(ctx, head)
    tokens = k_ref.shape[0]
    arrays = (
        (k_ref, lambda s: lines.at[0, x, cols(s, tokens)], D),
        (v_ref, lambda s: lines.at[1, y, cols(s, tokens)], D),
        (q_ref, lambda s: qh_ref.at[cols(s, tokens)], QW),
        (c_ref, lambda s: ch_ref.at[cols(s, tokens)], QW),
    )

    def at(kind, along, across):
        return across * SIDE + along if kind == 0 else along * SIDE + across

    def send(a, to, frm):
        ref, place, width = arrays[a]
        return pltpu.make_async_remote_copy(
            ref.at[:, cols(to, width)], place(frm), head_send.at[a, to], head_recv.at[a, frm],
            device_id=(ctx, to), device_id_type=MESH)

    def keep(a):
        ref, place, width = arrays[a]
        return pltpu.make_async_copy(ref.at[:, cols(head, width)], place(head), local_sem.at[a])

    def each_head(arrays_used, act):
        def one(n, _):
            peer = lax.rem(head + n, HEADS)
            for a in arrays_used:
                act(a, peer)
            return 0
        lax.fori_loop(1, HEADS, one, 0)

    for a in range(4):
        keep(a).start()
    each_head((0, 1), lambda a, p: send(a, p, head).start())
    each_head((2, 3), lambda a, p: send(a, p, head).start())
    keep(0).wait()
    keep(1).wait()
    each_head((0, 1), lambda a, p: send(a, p, p).wait_recv())

    def share(kind, to, frm):
        return pltpu.make_async_remote_copy(
            lines.at[kind, frm], lines.at[kind, frm], line_send.at[kind, to], line_recv.at[kind, frm],
            device_id=(at(kind, to, here[1 - kind]), head), device_id_type=MESH)

    def push(kind, to, along, frm):
        source = at(kind, along, frm)
        return pltpu.make_async_remote_copy(
            stage.at[kind, to, along], table_ref.at[source, :, kind * D:(kind + 1) * D],
            push_send.at[kind, to, along], push_recv.at[kind, frm, along],
            device_id=(at(kind, here[kind], to), head), device_id_type=MESH)

    def fill(kind, along):
        mine = here[1 - kind]
        return pltpu.make_async_copy(
            stage.at[kind, mine, along], table_ref.at[at(kind, along, mine), :, kind * D:(kind + 1) * D],
            fill_sem.at[kind, along])

    def own(kind, b):
        return pltpu.make_async_copy(
            lines.at[kind, here[kind], b * T:(b + 1) * T], table_ref.at[CTX + b, :, kind * D:(kind + 1) * D],
            local_sem.at[4 + 2 * kind + b])

    def prepare(kind, to, along):
        source = at(kind, along, here[1 - kind])
        second = lists_block(lists, at(kind, here[kind], to), 2 * source + 1)
        stage[kind, to, along] = jnp.where(second, lines[kind, along, T:], lines[kind, along, :T])

    for n in (1, 3, 2):
        for kind in range(2):
            share(kind, lax.rem(here[kind] + n, SIDE), here[kind]).start()
    for kind in range(2):
        for b in range(2):
            own(kind, b).start()

    def push_all(m, _):
        for kind in range(2):
            along = lax.rem(here[kind] + m, SIDE)

            @pl.when(m > 0)
            def _():
                share(kind, along, along).wait_recv()

            for n in range(1, SIDE):
                to = lax.rem(here[1 - kind] + n, SIDE)
                prepare(kind, to, along)
                push(kind, to, along, here[1 - kind]).start()

            @pl.when(m > 0)
            def _():
                prepare(kind, here[1 - kind], along)
                fill(kind, along).start()
        return 0

    lax.fori_loop(0, SIDE, push_all, 0)

    each_head(range(4), lambda a, p: send(a, p, head).wait_send())
    each_head((2, 3), lambda a, p: send(a, p, p).wait_recv())
    keep(2).wait()
    keep(3).wait()

    def drain(m, _):
        for kind in range(2):
            along = lax.rem(here[kind] + m, SIDE)

            @pl.when(m > 0)
            def _():
                share(kind, along, here[kind]).wait_send()
                fill(kind, along).wait()

            for n in range(1, SIDE):
                peer = lax.rem(here[1 - kind] + n, SIDE)
                push(kind, peer, along, here[1 - kind]).wait_send()
                push(kind, peer, along, peer).wait_recv()
        return 0

    lax.fori_loop(0, SIDE, drain, 0)
    for kind in range(2):
        for b in range(2):
            own(kind, b).wait()


def spread(lists, q, k, v, cot):
    bf = jnp.bfloat16
    any_spec = pl.BlockSpec(memory_space=pl.ANY)
    dma = pltpu.SemaphoreType.DMA
    return pl.pallas_call(
        spread_kernel,
        out_shape=(jax.ShapeDtypeStruct((2 * T, QW), bf), jax.ShapeDtypeStruct((2 * T, QW), bf),
                   jax.ShapeDtypeStruct((CTX + 2, T, 2 * D), bf)),
        in_specs=[pl.BlockSpec(memory_space=pltpu.SMEM)] + [any_spec] * 4,
        out_specs=(any_spec,) * 3,
        scratch_shapes=[
            pltpu.VMEM((2, SIDE, 2 * T, D), bf),
            pltpu.VMEM((2, SIDE, SIDE, T, D), bf),
            dma((4, HEADS)), dma((4, HEADS)), dma((2, SIDE)), dma((2, SIDE)),
            dma((2, SIDE, SIDE)), dma((2, SIDE, SIDE)), dma((8,)), dma((2, SIDE)),
        ],
        compiler_params=pltpu.CompilerParams(collective_id=0, has_side_effects=True, vmem_limit_bytes=60 * 2**20),
    )(lists, q, k, v, cot)


def collect_kernel(lists, out_ref, dq_ref, send_ref, own_ref, o_res, dq_res, dk_res, dv_res,
                   first, sums, second, total, grads,
                   head_send, head_recv, line_send, line_recv, push_send, push_recv, local_sem):
    f32, bf = jnp.float32, jnp.bfloat16
    ctx, head = lax.axis_index("ctx"), lax.axis_index("head")
    y, x = ctx // SIDE, lax.rem(ctx, SIDE)
    here = (x, y)
    greet(ctx, head)
    tokens = o_res.shape[0]
    arrays = (
        (lambda to: out_ref.at[cols(to, tokens)], lambda s: o_res.at[:, cols(s, QW)]),
        (lambda to: dq_ref.at[cols(to, tokens)], lambda s: dq_res.at[:, cols(s, QW)]),
        (lambda to: grads.at[0, cols(to, tokens)], lambda s: dk_res.at[:, cols(s, D)]),
        (lambda to: grads.at[1, cols(to, tokens)], lambda s: dv_res.at[:, cols(s, D)]),
    )

    def at(kind, along, across):
        return across * SIDE + along if kind == 0 else along * SIDE + across

    def part(kind, to):
        if kind == 0:
            return send_ref.at[:, to, :, :D]
        return send_ref.at[to, :, :, D:]

    def share(kind, to, frm):
        return pltpu.make_async_remote_copy(
            part(kind, to), first.at[kind, frm], line_send.at[kind, to], line_recv.at[kind, frm],
            device_id=(at(kind, to, here[1 - kind]), head), device_id_type=MESH)

    def hold(kind):
        return pltpu.make_async_copy(part(kind, here[kind]), first.at[kind, here[kind]], local_sem.at[4 + kind])

    def push(kind, to, frm):
        return pltpu.make_async_remote_copy(
            sums.at[kind, to], second.at[kind, frm], push_send.at[kind, to], push_recv.at[kind, frm],
            device_id=(at(kind, here[kind], to), head), device_id_type=MESH)

    def send(a, to, frm):
        source, place = arrays[a]
        return pltpu.make_async_remote_copy(
            source(to), place(frm), head_send.at[a, to], head_recv.at[a, frm],
            device_id=(ctx, to), device_id_type=MESH)

    def keep(a):
        source, place = arrays[a]
        return pltpu.make_async_copy(source(head), place(head), local_sem.at[a])

    def each_head(arrays_used, act):
        def one(n, _):
            peer = lax.rem(head + n, HEADS)
            for a in arrays_used:
                act(a, peer)
            return 0
        lax.fori_loop(1, HEADS, one, 0)

    for n in (1, 3, 2):
        for kind in range(2):
            share(kind, lax.rem(here[kind] + n, SIDE), here[kind]).start()
    for kind in range(2):
        hold(kind).start()
    each_head((0, 1), lambda a, p: send(a, p, head).start())
    keep(0).start()
    keep(1).start()
    start_total = pltpu.make_async_copy(own_ref, total, local_sem.at[6])
    start_total.start()
    for kind in range(2):
        hold(kind).wait()
        for n in range(1, SIDE):
            peer = lax.rem(here[kind] + n, SIDE)
            share(kind, peer, peer).wait_recv()

    def add_line(n, _):
        for kind in range(2):
            to = lax.rem(here[1 - kind] + n, SIDE)
            target = at(kind, here[kind], to)
            for b in range(2):
                acc = jnp.zeros((T, D), f32)
                for along in range(SIDE):
                    source = at(kind, along, here[1 - kind])
                    take = jnp.logical_and(lists_block(lists, source, 2 * target + b), source != target)
                    acc += jnp.where(take, first[kind, along, to].astype(f32), 0.0)
                sums[kind, to, b] = acc.astype(bf)

            @pl.when(n < SIDE)
            def _():
                push(kind, to, here[1 - kind]).start()
        return 0

    lax.fori_loop(1, SIDE + 1, add_line, 0)
    start_total.wait()
    for kind in range(2):
        for b in range(2):
            total[kind, b] += sums[kind, here[1 - kind], b].astype(f32)
        for n in range(1, SIDE):
            frm = lax.rem(here[1 - kind] + n, SIDE)
            push(kind, frm, frm).wait_recv()
            for b in range(2):
                total[kind, b] += second[kind, frm, b].astype(f32)
        for b in range(2):
            grads[kind, b * T:(b + 1) * T] = total[kind, b].astype(bf)

    each_head((2, 3), lambda a, p: send(a, p, head).start())
    keep(2).start()
    keep(3).start()
    for kind in range(2):
        for n in range(1, SIDE):
            share(kind, lax.rem(here[kind] + n, SIDE), here[kind]).wait_send()
            push(kind, lax.rem(here[1 - kind] + n, SIDE), here[1 - kind]).wait_send()
    each_head(range(4), lambda a, p: send(a, p, head).wait_send())
    each_head(range(4), lambda a, p: send(a, p, p).wait_recv())
    for a in range(4):
        keep(a).wait()


def collect(lists, out, dq, send, own):
    f32, bf = jnp.float32, jnp.bfloat16
    any_spec = pl.BlockSpec(memory_space=pl.ANY)
    tokens = 2 * T // HEADS
    wide = jax.ShapeDtypeStruct((tokens, HEADS * QW), bf)
    thin = jax.ShapeDtypeStruct((tokens, HEADS * D), bf)
    dma = pltpu.SemaphoreType.DMA
    return pl.pallas_call(
        collect_kernel,
        out_shape=(wide, wide, thin, thin),
        in_specs=[pl.BlockSpec(memory_space=pltpu.SMEM)] + [any_spec] * 4,
        out_specs=(any_spec,) * 4,
        scratch_shapes=[
            pltpu.VMEM((2, SIDE, SIDE, T, D), bf),
            pltpu.VMEM((2, SIDE, 2, T, D), bf),
            pltpu.VMEM((2, SIDE, 2, T, D), bf),
            pltpu.VMEM((2, 2, T, D), f32),
            pltpu.VMEM((2, 2 * T, D), bf),
            dma((4, HEADS)), dma((4, HEADS)), dma((2, SIDE)), dma((2, SIDE)),
            dma((2, SIDE)), dma((2, SIDE)), dma((7,)),
        ],
        compiler_params=pltpu.CompilerParams(collective_id=1, has_side_effects=True, vmem_limit_bytes=60 * 2**20),
    )(lists, out, dq, send, own)


def shards(input_queries, input_keys, input_values, cotangent, block_list, block_count):
    queries, cot, table = spread(block_list, input_queries, input_keys, input_values, cotangent)
    out, dq, send, own = attn(block_list, block_count, queries, cot, table)
    return collect(block_list, out, dq, send.reshape(SIDE, SIDE, T, 2 * D), own)


def solution(mesh):
    spec = P(("ctx", "head"), None)
    return jax.shard_map(
        shards,
        mesh=mesh,
        in_specs=(spec,) * 4 + (P(), P()),
        out_specs=(spec,) * 4,
        check_vma=False,
    )
```

time: 378 us -> 232 us (0.61)
  Pallas kernels: 74.8 us -> 224 us
  waiting for transfers between devices: 139 us -> 0 us
  starting transfers between devices: 83.1 us -> 0 us
  blocking collectives: 45.6 us -> 0 us
  between operations: 14.1 us -> 0.67 us
  local copies, waits for them, and re-layouts: 14.6 us -> 6.73 us
  other arithmetic: 5.8 us -> 0 us
    pallas_call x0 -> x2, Pallas kernels: none -> 149 us  [the longest x1 94.6 us: collect(): pl.pallas_call(collect_kernel, out_shape=(wide, wide, thin, thin), in_spe...]
    all_to_all x6 -> x0, waiting for transfers between devices: 122 us -> none  [the longest x1 60.9 us: shards(): got = lax.all_to_all(send, 'ctx', split_axis=0, concat_axis=0, tiled=True)]
    all_to_all x6 -> x0, starting transfers between devices: 83.1 us -> none  [the longest x1 55.7 us: shards(): got = lax.all_to_all(send, 'ctx', split_axis=0, concat_axis=0, tiled=True)]
    all_to_all x3 -> x0, blocking collectives: 45.6 us -> none  [the longest x2 35.6 us: heads_out(): lax.all_to_all(x.reshape(8, -1, width), 'head', split_axis=0, concat_axis...]
    all_gather x1 -> x0, waiting for transfers between devices: 17 us -> none  [shards(): table = lax.all_gather(own_table, 'ctx', axis=0, tiled=True)]
    reshape x6 -> x0, local copies, waits for them, and re-layouts: 6.68 us -> none  [the longest x2 4.02 us: heads_out(): return jnp.transpose(x, (1, 0, 2)).reshape(-1, 8 * width)]
    reduce_sum x1 -> x0, other arithmetic: 4.25 us -> none  [shards(): jnp.sum(parts.astype(jnp.float32), axis=0)]
  transfers between devices with their start and end apart: 7 -> 0, of which waited for: 7 -> 0; matrix products, arithmetic and copies ran while one was open for 4% -> 0% of each run, Pallas kernels for 0% -> 0%
where the time goes in v3:
time: 232 us
  Pallas kernels  224 us (97%)
  local copies, waits for them, and re-layouts  6.73 us (3%)
    pallas_call x1, Pallas kernels, collect(): pl.pallas_call(collect_kernel, out_shape=(wide, wide, thin, thin), in_spe...  94.6 us
    pallas_call x1, Pallas kernels, attn(): pl.pallas_call(attn_kernel, out_shape=(jax.ShapeDtypeStruct((2 * T, GROUP...  74.8 us
    pallas_call x1, Pallas kernels, spread(): pl.pallas_call(spread_kernel, out_shape=(jax.ShapeDtypeStruct((2 * T, QW)...  54.7 us
    unnamed x11, local copies, waits for them, and re-layouts  6.73 us

profile of v3, /device:TPU:1, one launch (start us, length us, event | category | flops | bytes accessed | tf_op | source)
XLA Modules:
  0.0 231.5 jit_solution(15311399895844387569)
XLA Ops:
  0.6 1.4 copy.12.lists
  2.0 54.7 %shard_map.93 = (bf16[1024,768]{1,0:T(8,128)(2,1)}, bf16[1024,768]{1,0:T(8,128)(2,1)}, bf16[18,512,256]{2,1,0:T(8,128)(2,1)}) custom-call(s32[32,8]{1,0:T(8,128)} %copy.12.lists, bf16[128,6144]{1,0:T(8,128)(2,1)} %q_ref.1, bf16[128,1024]{1,0:T(8,128)(2,1)} %k_ref.1, bf16[128,1024]{1,0:T(8,128)(2,1)} %v_ref.1, bf16[128,6144]{1,0:T(8,128)(2,1)} %c_ref.1), custom_call_target="tpu_custom_call" | custom-call | tf_op jit(solution)/shard_map/pallas_call | solution.py:279
  56.7 74.8 %shard_map.94 = (bf16[1024,768]{1,0:T(8,128)(2,1)}, bf16[1024,768]{1,0:T(8,128)(2,1)}, bf16[16,512,256]{2,1,0:T(8,128)(2,1)}, f32[2,2,512,128]{3,2,1,0:T(8,128)}) custom-call(s32[32,8]{1,0:T(8,128)} %copy.12.lists, s32[32]{0:T(128)} %counts.1, bf16[1024,768]{1,0:T(8,128)(2,1)} %get-tuple-element.11.q_ref, bf16[1024,768]{1,0:T(8,128)(2,1)} %get-tuple-element.12.cot_ref, ...), custom_call_target="tpu_custom_call" | custom-call | tf_op jit(solution)/shard_map/pallas_call | solution.py:110
  131.6 94.6 %shard_map.95 = (bf16[128,6144]{1,0:T(8,128)(2,1)}, bf16[128,6144]{1,0:T(8,128)(2,1)}, bf16[128,1024]{1,0:T(8,128)(2,1)}, bf16[128,1024]{1,0:T(8,128)(2,1)}) custom-call(s32[32,8]{1,0:T(8,128)} %copy.12.lists, bf16[1024,768]{1,0:T(8,128)(2,1)} %get-tuple-element.14.out_ref, bf16[1024,768]{1,0:T(8,128)(2,1)} %get-tuple-element.15.dq_ref, ...), custom_call_target="tpu_custom_call" | custom-call | tf_op jit(solution)/shard_map/pallas_call | solution.py:416
  226.1 0.0 copy-start
  226.1 2.8 %copy.17 = bf16[128,6144]{1,0:T(8,128)(2,1)} copy(bf16[128,6144]{1,0:T(8,128)(2,1)} %get-tuple-element.22) | data formatting | bytes 3145728
  229.0 0.0 copy-done
  229.0 0.0 copy-start.2
  229.0 0.0 copy-start.1
  229.0 1.1 copy.18
  230.1 0.0 copy-done.2
  230.1 0.7 copy.19
  230.8 0.0 copy-done.1
  230.8 0.7 copy.20
Async XLA Ops:
  226.1 2.8 %copy-start = (bf16[128,6144]{1,0:T(8,128)(2,1)S(1)}, bf16[128,6144]{1,0:T(8,128)(2,1)}, u32[]{:S(2)}) copy-start(bf16[128,6144]{1,0:T(8,128)(2,1)} %get-tuple-element.23) | copy-start | bytes 4718596
  229.0 1.1 copy-start.2
  229.0 1.9 copy-start.1

commit v4 on v3

--- a/solution.py
+++ b/solution.py
@@ -19,102 +19,198 @@
 MESH = pl.DeviceIdType.MESH
 
 
-def attn_kernel(lists, counts, q_ref, cot_ref, kv_hbm, out_ref, dq_ref, send_ref, own_ref,
-                kv, pst, mst, acc, run, dqa, sems):
+def attn_kernel(lists, counts, q_hbm, cot_hbm, kv_hbm, out_hbm, dq_hbm, send_hbm, own_hbm,
+                q, cot, kv, weights, acc, dqa, stat, scaled_t, scaled, out, dq, send, own,
+                kv_sem, in_sem, out_sem, send_sem):
+    f32, bf = jnp.float32, jnp.bfloat16
     ctx = lax.axis_index("ctx")
 
     def owner(b, i):
-        return lists[2 * ctx + b, i] // 2
-
-    f32=jnp.float32; bf=jnp.bfloat16
+        return lists[i, 2 * ctx + b] // 2
+
+    def named(b, block_owner):
+        hits = jnp.int32(0)
+        for n in range(1, MOST):
+            hits += (owner(b, n) == block_owner).astype(jnp.int32)
+        return hits > 0
+
+    def rows(b):
+        return pl.ds(b * T, T)
+
     def fetch(b, i):
         slot = jnp.where(i == 0, CTX + b, owner(b, i))
-        return pltpu.make_async_copy(kv_hbm.at[slot], kv.at[b * MOST + i], sems.at[b * MOST + i])
-
-    def prefetch(b):
+        return pltpu.make_async_copy(kv_hbm.at[slot], kv.at[b * MOST + i], kv_sem.at[b * MOST + i])
+
+    def load(b, a):
+        source, place = ((q_hbm, q), (cot_hbm, cot))[a]
+        return pltpu.make_async_copy(source.at[rows(b)], place.at[rows(b)], in_sem.at[b, a])
+
+    def store(b, a):
+        source, place = ((out, out_hbm), (dq, dq_hbm))[a]
+        return pltpu.make_async_copy(source.at[rows(b)], place.at[rows(b)], out_sem.at[b, a])
+
+    def store_own(b):
+        return pltpu.make_async_copy(own.at[:, b], own_hbm.at[:, b], out_sem.at[b, 2])
+
+    def store_send(d):
+        return pltpu.make_async_copy(send.at[d], send_hbm.at[d], send_sem.at[d])
+
+    def each_live(b, act, start=0):
         def one(i, _):
-            fetch(b, i).start()
+            act(i)
             return 0
-        lax.fori_loop(0, counts[2 * ctx + b], one, 0)
-
-    prefetch(0)
-    prefetch(1)
+        lax.fori_loop(start, counts[2 * ctx + b], one, 0)
+
     for b in range(2):
-        rows=slice(b*T,(b+1)*T)
-        cnt=counts[2*ctx+b]
-        acc[...]=jnp.zeros_like(acc)
-        run[0]=jnp.full((8,T),-1e30,f32)
-        run[1]=jnp.zeros((8,T),f32)
-        def fwd(i, _):
+        load(b, 0).start()
+        each_live(b, lambda i: fetch(b, i).start())
+        load(b, 1).start()
+
+    for b in range(2):
+        lo = b * T
+
+        def score(i, j):
+            return lax.dot_general(kv[b * MOST + i, :, :D], q[lo:lo + T, j * D:(j + 1) * D], NT,
+                                   preferred_element_type=f32)
+
+        def top(i):
+            for j in range(GROUP):
+                best = jnp.max(score(i, j), axis=0, keepdims=True) * (SCALE * LOG2E)
+                stat[0, j:j + 1] = jnp.maximum(stat[0, j:j + 1], best)
+
+        def attend(i, shifted):
+            values_t = kv[b * MOST + i, :, D:].T
+            for j in range(GROUP):
+                level = score(i, j) * (SCALE * LOG2E)
+                if shifted:
+                    level = level - stat[0, j:j + 1]
+                weight = jnp.exp2(level)
+                stat[1, j:j + 1] += jnp.sum(weight, axis=0, keepdims=True)
+                weight = weight.astype(bf)
+                weights[i, :, j * T:(j + 1) * T] = weight
+                acc[j] += jnp.dot(values_t, weight, preferred_element_type=f32)
+
+        def clear():
+            acc[...] = jnp.zeros_like(acc)
+            stat[1] = jnp.zeros((8, T), f32)
+
+        def attend_first(i):
             fetch(b, i).wait()
-            k=kv[b*8+i,:,:D]; vt=kv[b*8+i,:,D:].T
+            attend(i, False)
+
+        load(b, 0).wait()
+        clear()
+        each_live(b, attend_first)
+        sums = stat[1, :GROUP]
+        safe = jnp.logical_and(jnp.min(sums) > 2.0**-60, jnp.max(sums) < 2.0**60)
+
+        @pl.when(jnp.logical_not(safe))
+        def _():
+            stat[0] = jnp.full((8, T), -1e30, f32)
+            each_live(b, top)
+            clear()
+            each_live(b, lambda i: attend(i, True))
+
+        load(b, 1).wait()
+        for j in range(GROUP):
+            inverse = 1.0 / stat[1, j:j + 1]
+            attended = (acc[j] * inverse).astype(bf)
+            out[lo:lo + T, j * D:(j + 1) * D] = attended.T
+            cot_t = cot[lo:lo + T, j * D:(j + 1) * D].T.astype(f32)
+            stat[2, j:j + 1] = jnp.sum(attended.astype(f32) * cot_t, axis=0, keepdims=True) * inverse
+            part = (cot_t * inverse).astype(bf)
+            scaled_t[j] = part
+            scaled[j] = part.T
+        store(b, 0).start()
+        dqa[...] = jnp.zeros_like(dqa)
+
+        def back(i):
+            keys = kv[b * MOST + i, :, :D]
+            values = kv[b * MOST + i, :, D:]
+            keys_t = keys.T
+            dk = jnp.zeros((T, D), f32)
+            dv = jnp.zeros((T, D), f32)
             for j in range(GROUP):
-                qj=q_ref[rows,j*D:(j+1)*D]
-                s=lax.dot_general(k,qj,NT,preferred_element_type=f32)
-                mx=jnp.max(s,axis=0,keepdims=True)*(SCALE*LOG2E)
-                p=jnp.exp2(s*(SCALE*LOG2E)-mx)
-                li=jnp.sum(p,axis=0,keepdims=True)
-                pb=p.astype(bf)
-                pst[i,:,j*T:(j+1)*T]=pb
-                ot=jnp.dot(vt,pb,preferred_element_type=f32)
-                mo=run[0,j:j+1]; mn=jnp.maximum(mo,mx)
-                al=jnp.exp2(mo-mn); be=jnp.exp2(mx-mn)
-                mst[i,j:j+1]=mx
-                run[0,j:j+1]=mn
-                run[1,j:j+1]=run[1,j:j+1]*al+li*be
-                acc[j]=acc[j]*al+ot*be
-            return 0
-        lax.fori_loop(0,cnt,fwd,0)
+                change = jnp.dot(values, scaled_t[j], preferred_element_type=f32) - stat[2, j:j + 1]
+                weight = weights[i, :, j * T:(j + 1) * T]
+                ds = (weight.astype(f32) * change).astype(bf)
+                dqa[j] += jnp.dot(keys_t, ds, preferred_element_type=f32)
+                dk += jnp.dot(ds, q[lo:lo + T, j * D:(j + 1) * D], preferred_element_type=f32)
+                dv += jnp.dot(weight, scaled[j], preferred_element_type=f32)
+            dk = dk * SCALE
+            d = owner(b, i)
+            other = named(1 - b, d)
+
+            @pl.when(i == 0)
+            def _():
+                own[0, b] = dk
+                own[1, b] = dv
+
+            if b == 0:
+                @pl.when(i > 0)
+                def _():
+                    send[d, :, :D] = dk.astype(bf)
+                    send[d, :, D:] = dv.astype(bf)
+
+                @pl.when(jnp.logical_and(i > 0, jnp.logical_not(other)))
+                def _():
+                    store_send(d).start()
+            else:
+                @pl.when(jnp.logical_and(i > 0, jnp.logical_not(other)))
+                def _():
+                    send[d, :, :D] = dk.astype(bf)
+                    send[d, :, D:] = dv.astype(bf)
+
+                @pl.when(jnp.logical_and(i > 0, other))
+                def _():
+                    send[d, :, :D] = (send[d, :, :D].astype(f32) + dk).astype(bf)
+                    send[d, :, D:] = (send[d, :, D:].astype(f32) + dv).astype(bf)
+
+                @pl.when(i > 0)
+                def _():
+                    store_send(d).start()
+
+        each_live(b, back)
+        store_own(b).start()
         for j in range(GROUP):
-            o=(acc[j]/run[1,j:j+1]).astype(bf)
-            out_ref[rows,j*D:(j+1)*D]=o.T
-            ct=cot_ref[rows,j*D:(j+1)*D].T
-            run[2,j:j+1]=jnp.sum(o.astype(f32)*ct.astype(f32),axis=0,keepdims=True)
-        dqa[...]=jnp.zeros_like(dqa)
-        def bwd(i,_):
-            k=kv[b*8+i,:,:D]; v=kv[b*8+i,:,D:]; kt=k.T
-            dk=jnp.zeros((T,D),f32); dv=jnp.zeros((T,D),f32)
-            for j in range(GROUP):
-                qj=q_ref[rows,j*D:(j+1)*D]; cj=cot_ref[rows,j*D:(j+1)*D]
-                dp=lax.dot_general(v,cj,NT,preferred_element_type=f32)
-                r=jnp.exp2(mst[i,j:j+1]-run[0,j:j+1])/run[1,j:j+1]
-                pn=pst[i,:,j*T:(j+1)*T].astype(f32)*r
-                ds=(pn*(dp-run[2,j:j+1])).astype(bf)
-                dqa[j]+=jnp.dot(kt,ds,preferred_element_type=f32)
-                dk+=jnp.dot(ds,qj,preferred_element_type=f32)
-                dv+=jnp.dot(pn.astype(bf),cj,preferred_element_type=f32)
-            dk=dk*SCALE
-            d=owner(b, i)
-            sh=jnp.int32(0)
-            if b == 1:
-                for n in range(1, MOST):
-                    sh += (owner(0, n) == d).astype(jnp.int32)
-            @pl.when(i==0)
-            def _():
-                own_ref[0,b]=dk; own_ref[1,b]=dv
-            @pl.when(jnp.logical_and(i>0, sh==0))
-            def _():
-                send_ref[d,:,:D]=dk.astype(bf); send_ref[d,:,D:]=dv.astype(bf)
-            @pl.when(jnp.logical_and(i>0, sh!=0))
-            def _():
-                send_ref[d,:,:D]=(send_ref[d,:,:D].astype(f32)+dk).astype(bf)
-                send_ref[d,:,D:]=(send_ref[d,:,D:].astype(f32)+dv).astype(bf)
-            return 0
-        lax.fori_loop(0,cnt,bwd,0)
-        for j in range(GROUP):
-            dq_ref[rows,j*D:(j+1)*D]=(dqa[j]*SCALE).astype(bf).T
-
-def attn(lists,counts,q,cot,kvt):
-    f32=jnp.float32; bf=jnp.bfloat16
-    V=pl.BlockSpec(memory_space=pltpu.VMEM)
-    return pl.pallas_call(attn_kernel,
-        out_shape=(jax.ShapeDtypeStruct((2*T,GROUP*D),bf),)*2+(jax.ShapeDtypeStruct((16,T,2*D),bf),jax.ShapeDtypeStruct((2,2,T,D),f32)),
-        in_specs=[pl.BlockSpec(memory_space=pltpu.SMEM)]*2+[V,V,pl.BlockSpec(memory_space=pl.ANY)],
-        out_specs=(V,)*4,
-        scratch_shapes=[pltpu.VMEM((16,T,2*D),bf),pltpu.VMEM((8,T,GROUP*T),bf),pltpu.VMEM((8,8,T),f32),
-            pltpu.VMEM((GROUP,D,T),f32),pltpu.VMEM((3,8,T),f32),pltpu.VMEM((GROUP,D,T),f32),pltpu.SemaphoreType.DMA((16,))],
-        compiler_params=pltpu.CompilerParams(vmem_limit_bytes=62*1024*1024),
-        )(lists,counts,q,cot,kvt)
+            dq[lo:lo + T, j * D:(j + 1) * D] = (dqa[j] * SCALE).astype(bf).T
+        store(b, 1).start()
+
+    def end_first(i):
+        d = owner(0, i)
+
+        @pl.when(jnp.logical_not(named(1, d)))
+        def _():
+            store_send(d).wait()
+
+    each_live(0, end_first, 1)
+    each_live(1, lambda i: store_send(owner(1, i)).wait(), 1)
+    for b in range(2):
+        store(b, 0).wait()
+        store(b, 1).wait()
+        store_own(b).wait()
+
+
+def attn(lists, counts, q, cot, kv):
+    f32, bf = jnp.float32, jnp.bfloat16
+    any_spec = pl.BlockSpec(memory_space=pl.ANY)
+    dma = pltpu.SemaphoreType.DMA
+    return pl.pallas_call(
+        attn_kernel,
+        out_shape=(jax.ShapeDtypeStruct((2 * T, QW), bf), jax.ShapeDtypeStruct((2 * T, QW), bf),
+                   jax.ShapeDtypeStruct((CTX, T, 2 * D), bf), jax.ShapeDtypeStruct((2, 2, T, D), f32)),
+        in_specs=[pl.BlockSpec(memory_space=pltpu.SMEM)] * 2 + [any_spec] * 3,
+        out_specs=(any_spec,) * 4,
+        scratch_shapes=[
+            pltpu.VMEM((2 * T, QW), bf), pltpu.VMEM((2 * T, QW), bf), pltpu.VMEM((2 * MOST, T, 2 * D), bf),
+            pltpu.VMEM((MOST, T, GROUP * T), bf), pltpu.VMEM((GROUP, D, T), f32), pltpu.VMEM((GROUP, D, T), f32),
+            pltpu.VMEM((3, 8, T), f32), pltpu.VMEM((GROUP, D, T), bf), pltpu.VMEM((GROUP, T, D), bf),
+            pltpu.VMEM((2 * T, QW), bf), pltpu.VMEM((2 * T, QW), bf), pltpu.VMEM((CTX, T, 2 * D), bf),
+            pltpu.VMEM((2, 2, T, D), f32),
+            dma((2 * MOST,)), dma((2, 2)), dma((2, 3)), dma((CTX,)),
+        ],
+        compiler_params=pltpu.CompilerParams(vmem_limit_bytes=62 * 2**20),
+    )(lists, counts, q, cot, kv)
 
 
 def greet(ctx, head):
@@ -143,7 +239,7 @@
     hits = jnp.int32(0)
     for b in range(2):
         for i in range(1, MOST):
-            hits += (lists[2 * ctx + b, i] == block).astype(jnp.int32)
+            hits += (lists[i, 2 * ctx + b] == block).astype(jnp.int32)
     return hits > 0
 
 
@@ -432,9 +528,10 @@
 
 
 def shards(input_queries, input_keys, input_values, cotangent, block_list, block_count):
-    queries, cot, table = spread(block_list, input_queries, input_keys, input_values, cotangent)
-    out, dq, send, own = attn(block_list, block_count, queries, cot, table)
-    return collect(block_list, out, dq, send.reshape(SIDE, SIDE, T, 2 * D), own)
+    lists = block_list.T
+    queries, cot, table = spread(lists, input_queries, input_keys, input_values, cotangent)
+    out, dq, send, own = attn(lists, block_count, queries, cot, table)
+    return collect(lists, out, dq, send.reshape(SIDE, SIDE, T, 2 * D), own)
 
 
 def solution(mesh):

time: 232 us -> 259 us (1.12)
  Pallas kernels: 224 us -> 251 us
    pallas_call x1, Pallas kernels: 74.8 us -> 90.8 us  [attn(): pl.pallas_call(attn_kernel, out_shape=(jax.ShapeDtypeStruct((2 * T, QW),...]
    pallas_call x1, Pallas kernels: 94.6 us -> 106 us  [collect(): pl.pallas_call(collect_kernel, out_shape=(wide, wide, thin, thin), in_spe...]
    unnamed x11 -> x10, local copies, waits for them, and re-layouts: 6.73 us -> 5.37 us
where the time goes in v4:
time: 259 us; the launch traced here: 258 us
  Pallas kernels  251 us (97%)
  local copies, waits for them, and re-layouts  5.37 us (2%)
    pallas_call x1, Pallas kernels, collect(): pl.pallas_call(collect_kernel, out_shape=(wide, wide, thin, thin), in_spe...  106 us
    pallas_call x1, Pallas kernels, attn(): pl.pallas_call(attn_kernel, out_shape=(jax.ShapeDtypeStruct((2 * T, QW),...  90.8 us
    pallas_call x1, Pallas kernels, spread(): pl.pallas_call(spread_kernel, out_shape=(jax.ShapeDtypeStruct((2 * T, QW)...  54.6 us
    unnamed x10, local copies, waits for them, and re-layouts  5.37 us

profile of v4, /device:TPU:1, one launch (start us, length us, event | category | flops | bytes accessed | tf_op | source)
XLA Modules:
  0.0 257.5 jit_solution(17901431057841882170)
XLA Ops:
  0.6 54.6 %shard_map.93 = (bf16[1024,768]{1,0:T(8,128)(2,1)}, bf16[1024,768]{1,0:T(8,128)(2,1)}, bf16[18,512,256]{2,1,0:T(8,128)(2,1)}) custom-call(s32[8,32]{1,0:T(8,128)} %bitcast.3, bf16[128,6144]{1,0:T(8,128)(2,1)} %q_ref.1, bf16[128,1024]{1,0:T(8,128)(2,1)} %k_ref.1, bf16[128,1024]{1,0:T(8,128)(2,1)} %v_ref.1, bf16[128,6144]{1,0:T(8,128)(2,1)} %c_ref.1), custom_call_target="tpu_custom_call" | custom-call | tf_op jit(solution)/shard_map/pallas_call | solution.py:375
  55.2 90.8 %shard_map.94 = (bf16[1024,768]{1,0:T(8,128)(2,1)}, bf16[1024,768]{1,0:T(8,128)(2,1)}, bf16[16,512,256]{2,1,0:T(8,128)(2,1)}, f32[2,2,512,128]{3,2,1,0:T(8,128)}) custom-call(s32[8,32]{1,0:T(8,128)} %bitcast.4, s32[32]{0:T(128)} %counts.1, bf16[1024,768]{1,0:T(8,128)(2,1)} %get-tuple-element.11.q_hbm, bf16[1024,768]{1,0:T(8,128)(2,1)} %get-tuple-element.12.cot_hbm, ...), custom_call_target="tpu_custom_call" | custom-call | tf_op jit(solution)/shard_map/pallas_call | solution.py:198
  146.0 106.1 %shard_map.95 = (bf16[128,6144]{1,0:T(8,128)(2,1)}, bf16[128,6144]{1,0:T(8,128)(2,1)}, bf16[128,1024]{1,0:T(8,128)(2,1)}, bf16[128,1024]{1,0:T(8,128)(2,1)}) custom-call(s32[8,32]{1,0:T(8,128)} %bitcast.5, bf16[1024,768]{1,0:T(8,128)(2,1)} %get-tuple-element.14.out_ref, bf16[1024,768]{1,0:T(8,128)(2,1)} %get-tuple-element.15.dq_ref, ...), custom_call_target="tpu_custom_call" | custom-call | tf_op jit(solution)/shard_map/pallas_call | solution.py:512
  252.1 0.0 copy-start
  252.2 2.8 %copy.14 = bf16[128,6144]{1,0:T(8,128)(2,1)} copy(bf16[128,6144]{1,0:T(8,128)(2,1)} %get-tuple-element.22) | data formatting | bytes 3145728
  255.0 0.0 copy-done
  255.0 0.0 copy-start.2
  255.0 0.0 copy-start.1
  255.0 1.1 copy.15
  256.1 0.0 copy-done.2
  256.1 0.7 copy.16
  256.8 0.0 copy-done.1
  256.8 0.7 copy.17
Async XLA Ops:
  252.1 2.8 %copy-start = (bf16[128,6144]{1,0:T(8,128)(2,1)S(1)}, bf16[128,6144]{1,0:T(8,128)(2,1)}, u32[]{:S(2)}) copy-start(bf16[128,6144]{1,0:T(8,128)(2,1)} %get-tuple-element.23) | copy-start | bytes 4718596
  255.0 1.1 copy-start.2
  255.0 1.9 copy-start.1

commit v5 on v4

--- a/solution.py
+++ b/solution.py
@@ -21,7 +21,7 @@
 
 def attn_kernel(lists, counts, q_hbm, cot_hbm, kv_hbm, out_hbm, dq_hbm, send_hbm, own_hbm,
                 q, cot, kv, weights, acc, dqa, stat, scaled_t, scaled, out, dq, send, own,
-                kv_sem, in_sem, out_sem, send_sem):
+                dscore, qs, kv_sem, in_sem, out_sem, send_sem):
     f32, bf = jnp.float32, jnp.bfloat16
     ctx = lax.axis_index("ctx")
 
@@ -86,9 +86,9 @@
                     level = level - stat[0, j:j + 1]
                 weight = jnp.exp2(level)
                 stat[1, j:j + 1] += jnp.sum(weight, axis=0, keepdims=True)
-                weight = weight.astype(bf)
-                weights[i, :, j * T:(j + 1) * T] = weight
-                acc[j] += jnp.dot(values_t, weight, preferred_element_type=f32)
+                weights[i, :, j * T:(j + 1) * T] = weight.astype(bf)
+            for j in range(GROUP):
+                acc[j] += jnp.dot(values_t, weights[i, :, j * T:(j + 1) * T], preferred_element_type=f32)
 
         def clear():
             acc[...] = jnp.zeros_like(acc)
@@ -123,6 +123,8 @@
             scaled[j] = part.T
         store(b, 0).start()
         dqa[...] = jnp.zeros_like(dqa)
+        for j in range(GROUP):
+            qs[j * T:(j + 1) * T] = q[lo:lo + T, j * D:(j + 1) * D]
 
         def back(i):
             keys = kv[b * MOST + i, :, :D]
@@ -133,10 +135,11 @@
             for j in range(GROUP):
                 change = jnp.dot(values, scaled_t[j], preferred_element_type=f32) - stat[2, j:j + 1]
                 weight = weights[i, :, j * T:(j + 1) * T]
-                ds = (weight.astype(f32) * change).astype(bf)
-                dqa[j] += jnp.dot(keys_t, ds, preferred_element_type=f32)
-                dk += jnp.dot(ds, q[lo:lo + T, j * D:(j + 1) * D], preferred_element_type=f32)
-                dv += jnp.dot(weight, scaled[j], preferred_element_type=f32)
+                dscore[:, j * T:(j + 1) * T] = (weight.astype(f32) * change).astype(bf)
+            for j in range(GROUP):
+                dqa[j] += jnp.dot(keys_t, dscore[:, j * T:(j + 1) * T], preferred_element_type=f32)
+            dv = jnp.dot(weights[i], scaled[...].reshape(GROUP * T, D), preferred_element_type=f32)
+            dk = jnp.dot(dscore[...], qs[...], preferred_element_type=f32)
             dk = dk * SCALE
             d = owner(b, i)
             other = named(1 - b, d)
@@ -207,6 +210,7 @@
             pltpu.VMEM((3, 8, T), f32), pltpu.VMEM((GROUP, D, T), bf), pltpu.VMEM((GROUP, T, D), bf),
             pltpu.VMEM((2 * T, QW), bf), pltpu.VMEM((2 * T, QW), bf), pltpu.VMEM((CTX, T, 2 * D), bf),
             pltpu.VMEM((2, 2, T, D), f32),
+            pltpu.VMEM((T, GROUP * T), bf), pltpu.VMEM((GROUP * T, D), bf),
             dma((2 * MOST,)), dma((2, 2)), dma((2, 3)), dma((CTX,)),
         ],
         compiler_params=pltpu.CompilerParams(vmem_limit_bytes=62 * 2**20),
@@ -527,11 +531,37 @@
     )(lists, out, dq, send, own)
 
 
+def finish_kernel(o_ref, dq_ref, dk_ref, dv_ref, o_res, dq_res, dk_res, dv_res, sem):
+    copies = []
+    for pair in ((o_ref, o_res), (dq_ref, dq_res)):
+        for n in range(4):
+            copies.append((pair, pl.ds(n * 32, 32)))
+    for pair in ((dk_ref, dk_res), (dv_ref, dv_res)):
+        copies.append((pair, pl.ds(0, 128)))
+    copies = [pltpu.make_async_copy(pair[0].at[rows], pair[1].at[rows], sem.at[n])
+              for n, (pair, rows) in enumerate(copies)]
+    for copy in copies:
+        copy.start()
+    for copy in copies:
+        copy.wait()
+
+
+def finish(arrays):
+    any_spec = pl.BlockSpec(memory_space=pl.ANY)
+    return pl.pallas_call(
+        finish_kernel,
+        out_shape=tuple(jax.ShapeDtypeStruct(a.shape, a.dtype) for a in arrays),
+        in_specs=[any_spec] * 4,
+        out_specs=(any_spec,) * 4,
+        scratch_shapes=[pltpu.SemaphoreType.DMA((10,))],
+    )(*arrays)
+
+
 def shards(input_queries, input_keys, input_values, cotangent, block_list, block_count):
     lists = block_list.T
     queries, cot, table = spread(lists, input_queries, input_keys, input_values, cotangent)
     out, dq, send, own = attn(lists, block_count, queries, cot, table)
-    return collect(lists, out, dq, send.reshape(SIDE, SIDE, T, 2 * D), own)
+    return finish(collect(lists, out, dq, send.reshape(SIDE, SIDE, T, 2 * D), own))
 
 
 def solution(mesh):

time: 259 us -> 321 us (1.24)
  Pallas kernels: 251 us -> 317 us
  local copies, waits for them, and re-layouts: 5.37 us -> 0 us
    pallas_call x0 -> x1, Pallas kernels: none -> 112 us  [finish(): pl.pallas_call(finish_kernel, out_shape=tuple((jax.ShapeDtypeStruct(a.sha...]
    pallas_call x1, Pallas kernels: 106 us -> 64.5 us  [collect(): pl.pallas_call(collect_kernel, out_shape=(wide, wide, thin, thin), in_spe...]
    unnamed x10 -> x0, local copies, waits for them, and re-layouts: 5.37 us -> none
    pallas_call x1, Pallas kernels: 90.8 us -> 85.9 us  [attn(): pl.pallas_call(attn_kernel, out_shape=(jax.ShapeDtypeStruct((2 * T, QW),...]
where the time goes in v5:
time: 321 us; the launch traced here: 318 us
  Pallas kernels  317 us (99%)
    pallas_call x1, Pallas kernels, finish(): pl.pallas_call(finish_kernel, out_shape=tuple((jax.ShapeDtypeStruct(a.sha...  112 us
    pallas_call x1, Pallas kernels, attn(): pl.pallas_call(attn_kernel, out_shape=(jax.ShapeDtypeStruct((2 * T, QW),...  85.9 us
    pallas_call x1, Pallas kernels, collect(): pl.pallas_call(collect_kernel, out_shape=(wide, wide, thin, thin), in_spe...  64.5 us
    pallas_call x1, Pallas kernels, spread(): pl.pallas_call(spread_kernel, out_shape=(jax.ShapeDtypeStruct((2 * T, QW)...  54.6 us

profile of v5, /device:TPU:1, one launch (start us, length us, event | category | flops | bytes accessed | tf_op | source)
XLA Modules:
  0.0 318.2 jit_solution(15262378628106761060)
XLA Ops:
  0.6 54.6 %shard_map.93 = (bf16[1024,768]{1,0:T(8,128)(2,1)}, bf16[1024,768]{1,0:T(8,128)(2,1)}, bf16[18,512,256]{2,1,0:T(8,128)(2,1)}) custom-call(s32[8,32]{1,0:T(8,128)} %bitcast.3, bf16[128,6144]{1,0:T(8,128)(2,1)} %q_ref.1, bf16[128,1024]{1,0:T(8,128)(2,1)} %k_ref.1, bf16[128,1024]{1,0:T(8,128)(2,1)} %v_ref.1, bf16[128,6144]{1,0:T(8,128)(2,1)} %c_ref.1), custom_call_target="tpu_custom_call" | custom-call | tf_op jit(solution)/shard_map/pallas_call | solution.py:379
  55.2 85.9 %shard_map.94 = (bf16[1024,768]{1,0:T(8,128)(2,1)}, bf16[1024,768]{1,0:T(8,128)(2,1)}, bf16[16,512,256]{2,1,0:T(8,128)(2,1)}, f32[2,2,512,128]{3,2,1,0:T(8,128)}) custom-call(s32[8,32]{1,0:T(8,128)} %bitcast.4, s32[32]{0:T(128)} %counts.1, bf16[1024,768]{1,0:T(8,128)(2,1)} %get-tuple-element.15.q_hbm, bf16[1024,768]{1,0:T(8,128)(2,1)} %get-tuple-element.16.cot_hbm, ...), custom_call_target="tpu_custom_call" | custom-call | tf_op jit(solution)/shard_map/pallas_call | solution.py:201
  141.1 64.5 %shard_map.95 = (bf16[128,6144]{1,0:T(8,128)(2,1)}, bf16[128,6144]{1,0:T(8,128)(2,1)}, bf16[128,1024]{1,0:T(8,128)(2,1)}, bf16[128,1024]{1,0:T(8,128)(2,1)}) custom-call(s32[8,32]{1,0:T(8,128)} %bitcast.5, bf16[1024,768]{1,0:T(8,128)(2,1)} %get-tuple-element.18.out_ref, bf16[1024,768]{1,0:T(8,128)(2,1)} %get-tuple-element.19.dq_ref, ...), custom_call_target="tpu_custom_call" | custom-call | tf_op jit(solution)/shard_map/pallas_call | solution.py:516
  205.6 112.4 %shard_map.96 = (bf16[128,6144]{1,0:T(8,128)(2,1)}, bf16[128,6144]{1,0:T(8,128)(2,1)}, bf16[128,1024]{1,0:T(8,128)(2,1)}, bf16[128,1024]{1,0:T(8,128)(2,1)}) custom-call(bf16[128,6144]{1,0:T(8,128)(2,1)} %get-tuple-element.22.o_ref, bf16[128,6144]{1,0:T(8,128)(2,1)} %get-tuple-element.23.dq_ref, bf16[128,1024]{1,0:T(8,128)(2,1)} %get-tuple-element.24.dk_ref, ...), custom_call_target="tpu_custom_call" | custom-call | tf_op jit(solution)/shard_map/pallas_call | solution.py:551

commit v6 on v5

--- a/solution.py
+++ b/solution.py
@@ -531,19 +531,23 @@
     )(lists, out, dq, send, own)
 
 
-def finish_kernel(o_ref, dq_ref, dk_ref, dv_ref, o_res, dq_res, dk_res, dv_res, sem):
-    copies = []
-    for pair in ((o_ref, o_res), (dq_ref, dq_res)):
-        for n in range(4):
-            copies.append((pair, pl.ds(n * 32, 32)))
-    for pair in ((dk_ref, dk_res), (dv_ref, dv_res)):
-        copies.append((pair, pl.ds(0, 128)))
-    copies = [pltpu.make_async_copy(pair[0].at[rows], pair[1].at[rows], sem.at[n])
-              for n, (pair, rows) in enumerate(copies)]
-    for copy in copies:
-        copy.start()
-    for copy in copies:
-        copy.wait()
+def finish_kernel(o_ref, dq_ref, dk_ref, dv_ref, o_res, dq_res, dk_res, dv_res, wide, thin, in_sem, out_sem):
+    moves = []
+    for n in range(8):
+        moves.append(((o_ref, dq_ref)[n % 2], wide.at[n % 2], (o_res, dq_res)[n % 2], pl.ds(n // 2 * 32, 32)))
+    for n in range(2):
+        moves.append(((dk_ref, dv_ref)[n], thin.at[n], (dk_res, dv_res)[n], pl.ds(0, 128)))
+    reads = [pltpu.make_async_copy(source.at[rows], held.at[rows], in_sem.at[n])
+             for n, (source, held, _, rows) in enumerate(moves)]
+    writes = [pltpu.make_async_copy(held.at[rows], target.at[rows], out_sem.at[n])
+              for n, (_, held, target, rows) in enumerate(moves)]
+    for read in reads:
+        read.start()
+    for read, write in zip(reads, writes):
+        read.wait()
+        write.start()
+    for write in writes:
+        write.wait()
 
 
 def finish(arrays):
@@ -553,7 +557,9 @@
         out_shape=tuple(jax.ShapeDtypeStruct(a.shape, a.dtype) for a in arrays),
         in_specs=[any_spec] * 4,
         out_specs=(any_spec,) * 4,
-        scratch_shapes=[pltpu.SemaphoreType.DMA((10,))],
+        scratch_shapes=[pltpu.VMEM((2, 128, HEADS * QW), jnp.bfloat16), pltpu.VMEM((2, 128, HEADS * D), jnp.bfloat16),
+                        pltpu.SemaphoreType.DMA((10,)), pltpu.SemaphoreType.DMA((10,))],
+        compiler_params=pltpu.CompilerParams(vmem_limit_bytes=60 * 2**20),
     )(*arrays)
 
 

time: 321 us -> 204 us (0.64)
  Pallas kernels: 317 us -> 201 us
    pallas_call x1, Pallas kernels: 112 us -> 3.07 us  [finish(): pl.pallas_call(finish_kernel, out_shape=tuple((jax.ShapeDtypeStruct(a.sha...]
    pallas_call x1, Pallas kernels: 85.9 us -> 78.7 us  [attn(): pl.pallas_call(attn_kernel, out_shape=(jax.ShapeDtypeStruct((2 * T, QW),...]
where the time goes in v6:
time: 204 us; the launch traced here: 202 us
  Pallas kernels  201 us (99%)
    pallas_call x1, Pallas kernels, attn(): pl.pallas_call(attn_kernel, out_shape=(jax.ShapeDtypeStruct((2 * T, QW),...  78.7 us
    pallas_call x1, Pallas kernels, collect(): pl.pallas_call(collect_kernel, out_shape=(wide, wide, thin, thin), in_spe...  64.5 us
    pallas_call x1, Pallas kernels, spread(): pl.pallas_call(spread_kernel, out_shape=(jax.ShapeDtypeStruct((2 * T, QW)...  54.6 us

profile of v6, /device:TPU:1, one launch (start us, length us, event | category | flops | bytes accessed | tf_op | source)
XLA Modules:
  0.0 201.6 jit_solution(16549069624795663696)
XLA Ops:
  0.6 54.6 %shard_map.93 = (bf16[1024,768]{1,0:T(8,128)(2,1)}, bf16[1024,768]{1,0:T(8,128)(2,1)}, bf16[18,512,256]{2,1,0:T(8,128)(2,1)}) custom-call(s32[8,32]{1,0:T(8,128)} %bitcast.3, bf16[128,6144]{1,0:T(8,128)(2,1)} %q_ref.1, bf16[128,1024]{1,0:T(8,128)(2,1)} %k_ref.1, bf16[128,1024]{1,0:T(8,128)(2,1)} %v_ref.1, bf16[128,6144]{1,0:T(8,128)(2,1)} %c_ref.1), custom_call_target="tpu_custom_call" | custom-call | tf_op jit(solution)/shard_map/pallas_call | solution.py:379
  55.2 78.7 %shard_map.94 = (bf16[1024,768]{1,0:T(8,128)(2,1)}, bf16[1024,768]{1,0:T(8,128)(2,1)}, bf16[16,512,256]{2,1,0:T(8,128)(2,1)}, f32[2,2,512,128]{3,2,1,0:T(8,128)}) custom-call(s32[8,32]{1,0:T(8,128)} %bitcast.4, s32[32]{0:T(128)} %counts.1, bf16[1024,768]{1,0:T(8,128)(2,1)} %get-tuple-element.15.q_hbm, bf16[1024,768]{1,0:T(8,128)(2,1)} %get-tuple-element.16.cot_hbm, ...), custom_call_target="tpu_custom_call" | custom-call | tf_op jit(solution)/shard_map/pallas_call | solution.py:201
  133.9 64.5 %shard_map.95 = (bf16[128,6144]{1,0:T(8,128)(2,1)}, bf16[128,6144]{1,0:T(8,128)(2,1)}, bf16[128,1024]{1,0:T(8,128)(2,1)}, bf16[128,1024]{1,0:T(8,128)(2,1)}) custom-call(s32[8,32]{1,0:T(8,128)} %bitcast.5, bf16[1024,768]{1,0:T(8,128)(2,1)} %get-tuple-element.18.out_ref, bf16[1024,768]{1,0:T(8,128)(2,1)} %get-tuple-element.19.dq_ref, ...), custom_call_target="tpu_custom_call" | custom-call | tf_op jit(solution)/shard_map/pallas_call | solution.py:516
  198.4 3.1 %shard_map.96 = (bf16[128,6144]{1,0:T(8,128)(2,1)}, bf16[128,6144]{1,0:T(8,128)(2,1)}, bf16[128,1024]{1,0:T(8,128)(2,1)}, bf16[128,1024]{1,0:T(8,128)(2,1)}) custom-call(bf16[128,6144]{1,0:T(8,128)(2,1)} %get-tuple-element.22.o_ref, bf16[128,6144]{1,0:T(8,128)(2,1)} %get-tuple-element.23.dq_ref, bf16[128,1024]{1,0:T(8,128)(2,1)} %get-tuple-element.24.dk_ref, ...), custom_call_target="tpu_custom_call" | custom-call | tf_op jit(solution)/shard_map/pallas_call | solution.py:555
